TPU v7x, 128 devices: a whole 4x4x4 slice. The times are simulated.
128 devices in a mesh: seq: 8 (over y, z_lo), dp: 16 (over x, z_hi, core).
Axes of the slice: x: 4, y: 4, z: 4 (z_hi: 2, z_lo: 2; z = z_hi * 2 + z_lo), core: 2. Of those that a mesh axis runs over, the one named last changes fastest.
Arguments:
- frames: bfloat16 [16, 2048, 1024], P('dp', 'seq'), may hold values from -6 to 6
- layernorm_gain: float32 [1024], replicated, may hold values from 0.25 to 1.75
- w_qkv: bfloat16 [1024, 3072], replicated
- w_out: bfloat16 [1024, 1024], replicated, may hold values from -0.1875 to 0.1875
- segment_ids: int32 [16, 2048], P('dp'), may hold values from 0 to 2, never falling along the last dimension, each value on 1 to 1536 neighbouring positions
- output_gradient: bfloat16 [16, 2048, 1024], P('dp', 'seq'), may hold values from -6 to 6
Outputs:
- layer_out: bfloat16 [16, 2048, 1024], P('dp', 'seq')
- frame_gradient: bfloat16 [16, 2048, 1024], P('dp', 'seq')
- grad_wqkv: bfloat16 [1024, 3072], P(('seq', 'dp'))
- grad_wout: bfloat16 [1024, 1024], P(('seq', 'dp'))
- grad_gain: float32 [1024], replicated
Inputs may be any that keep to these rules, and one draw needn't show every extreme that they name: `segment_ids`: frames of one recording are contiguous and numbered in order in each group; a recording has at most 1536 frames.
All inputs are finite; a program needn't handle non-finite values.
Results may differ from a plain program's by a relative error of at most 0.0095.
Values may be sent and summed in bfloat16 or wider, within the bound.
No kernel may reach another device: no remote copies, remote signals or barrier semaphores. Data moves between devices by JAX's collectives and lax.ppermute only.
A program may use at most 192 MiB of HBM per device.

v0:
```python
import functools

import jax
import jax.numpy as jnp
from jax import lax
from jax.experimental import pallas as pl
from jax.experimental.pallas import tpu as pltpu
from jax.sharding import PartitionSpec as P

HEADS = 8
BF = jnp.bfloat16
F32 = jnp.float32
LOG2E = 1.4426950408889634
PAIR = 4
CHUNK = 256
VMEM_LIMIT = 60 * 1024 * 1024
WHOLE = pl.BlockSpec(memory_space=pltpu.VMEM)
SCALARS = pl.BlockSpec(memory_space=pltpu.SMEM)


def seq_swap(x, bits):
    return lax.ppermute(x, "seq", [(i, i ^ bits) for i in range(8)])


def dp_swap(x, bits):
    return lax.ppermute(x, "dp", [(i, i ^ bits) for i in range(16)])


def seq_exchange(x):
    return lax.all_to_all(x, "seq", 0, 0, tiled=True)


def mm(a, b, ca, cb):
    return lax.dot_general(a, b, (((ca,), (cb,)), ((), ())), preferred_element_type=F32)


def call(kernel, name, out_shape, vmem=VMEM_LIMIT, **options):
    return pl.pallas_call(
        kernel,
        out_shape=out_shape,
        compiler_params=pltpu.CompilerParams(vmem_limit_bytes=vmem),
        name=name,
        **options,
    )


def shape(dtype, *dims):
    return jax.ShapeDtypeStruct(dims, dtype)


def layernorm(x):
    center = x - jnp.mean(x, axis=-1, keepdims=True)
    rstd = lax.rsqrt(jnp.mean(center * center, axis=-1, keepdims=True) + 1e-05)
    return center * rstd, rstd


def staged(
    body, name, out_shape, scalars, arrays, plain=(), left=(), scratch=(), vmem=VMEM_LIMIT
):
    n, m, k = len(scalars), len(arrays), len(plain) + len(left)

    def kernel(*refs):
        sources, others = refs[n : n + m], refs[n + m : n + m + k]
        outs = refs[n + m + k : n + m + k + len(out_shape)]
        rest = refs[n + m + k + len(out_shape) :]
        buffers, semaphores, rest = rest[:m], rest[m], rest[m + 1 :]
        copies = [
            pltpu.make_async_copy(sources[i], buffers[i], semaphores.at[i]) for i in range(m)
        ]
        for copy in copies:
            copy.start()
        waited = set()

        def get(i):
            if i not in waited:
                waited.add(i)
                copies[i].wait()
            return buffers[i]

        body(*refs[:n], get, *others, *outs, *rest)
        for i in range(m):
            get(i)

    return call(
        kernel,
        name,
        tuple(out_shape),
        vmem,
        in_specs=[SCALARS] * n
        + [pl.BlockSpec(memory_space=pltpu.HBM)] * m
        + [WHOLE] * len(plain)
        + [pl.BlockSpec(memory_space=pltpu.HBM)] * len(left),
        out_specs=(WHOLE,) * len(out_shape),
        scratch_shapes=[pltpu.VMEM(a.shape, a.dtype) for a in arrays]
        + [pltpu.SemaphoreType.DMA((m,))]
        + list(scratch),
    )(*scalars, *arrays, *plain, *left)


def layernorm_kernel(frames, gain, normed):
    xhat, _ = layernorm(frames[...].astype(F32))
    normed[...] = (xhat * gain[...]).astype(BF)


def dattn_kernel(pos, get, w_qkv, dattn, w_head, semaphores):
    copies = []
    for t in range(3):
        start = pl.multiple_of(t * 1024 + pos[0] * 128, 128)
        copies.append(
            pltpu.make_async_copy(
                w_qkv.at[:, pl.ds(start, 128)],
                w_head.at[:, t * 128 : (t + 1) * 128],
                semaphores.at[t],
            )
        )
    for copy in copies:
        copy.start()
    full = mm(get(0)[...], get(1)[...], 1, 1).astype(BF)
    for h in range(HEADS):
        dattn[h] = full[:, h * 128 : (h + 1) * 128]
    for copy in copies:
        copy.wait()


def attention_kernel(scale, places, pos, *refs):
    count = len(places)
    parts, (dout, ids) = refs[:count], refs[count : count + 2]
    attn, dqkv, q_s, k_s, v_s, kt_s, vt_s, dk_s, dv_s, s_s, p_s, l_s = refs[count + 2 :]
    rows = dout.shape[1]
    for part, (r, offset) in zip(parts, places):
        size = part.shape[0]
        rng = pl.ds(pl.multiple_of((pos[0] ^ r) * rows + offset, size), size)
        q_s[rng, :128] = part[:, :128]
        k_s[rng, :128] = part[:, 128:256]
        v_s[rng, :] = part[:, 256:]
    names = lax.broadcasted_iota(jnp.int32, (128, 8 * rows), 0)
    same = jnp.where(ids[...] == names, 1.0, 0.0).T
    q_s[:, 128:] = ((same - 1.0) * 1e30).astype(BF)
    k_s[:, 128:] = same.astype(BF)
    kt_s[...] = k_s[:, :128].T
    vt_s[...] = v_s[...].T
    dk_s[...] = jnp.zeros_like(dk_s)
    dv_s[...] = jnp.zeros_like(dv_s)

    size = min(CHUNK, 8 * rows)
    chunks = [slice(c, c + size) for c in range(0, 8 * rows, size)]

    def step(i, carry):
        for u in range(PAIR):
            block = i * PAIR + u
            rng = pl.ds(pl.multiple_of(block * rows, rows), rows)
            q, do, slot = q_s[rng, :], dout[block], u % 2
            peak = None
            for part in chunks:
                scores = mm(k_s[part, :], q, 1, 1)
                s_s[slot, part, :] = scores
                top = jnp.max(scores.reshape(-1, 8, rows), axis=0)
                peak = top if peak is None else jnp.maximum(peak, top)
            peak = jnp.max(peak, axis=0, keepdims=True)
            total = None
            for part in chunks:
                p_s[slot, part, :] = mm(v_s[part, :], do, 1, 1)
                expo = jnp.exp2((s_s[slot, part, :] - peak) * (scale * LOG2E))
                s_s[slot, part, :] = expo
                add = jnp.sum(expo.reshape(-1, 8, rows), axis=0)
                total = add if total is None else total + add
            inverse = 1.0 / jnp.sum(total, axis=0, keepdims=True)
            out = None
            for part in chunks:
                low = (s_s[slot, part, :] * inverse).astype(BF)
                l_s[slot, part, :] = low
                add = mm(vt_s[:, part], low, 1, 0)
                out = add if out is None else out + add
                dv_s[part, :] += mm(low, do, 1, 0)
            delta = jnp.sum(out * do.astype(F32).T, axis=0, keepdims=True)
            dq = None
            for part in chunks:
                dscores = l_s[slot, part, :].astype(F32) * (p_s[slot, part, :] - delta)
                dscores = dscores.astype(BF)
                dk_s[part, :] += mm(dscores, q[:, :128], 1, 0)
                add = mm(kt_s[:, part], dscores, 1, 0)
                dq = add if dq is None else dq + add
            attn[rng, :] = out.T.astype(BF)
            dqkv[rng, :128] = (dq * scale).T.astype(BF)
        return carry

    lax.fori_loop(0, 8 // PAIR, step, 0)
    dqkv[:, 128:256] = (dk_s[...] * scale).astype(BF)
    dqkv[:, 256:] = dv_s[...].astype(BF)


def attention(pos, parts, places, dout, ids, scale):
    total = ids.shape[1]
    return call(
        functools.partial(attention_kernel, scale, places),
        "attention",
        (shape(BF, total, 128), shape(BF, total, 384)),
        vmem=48 * 1024 * 1024,
        in_specs=[SCALARS] + [WHOLE] * (len(parts) + 2),
        out_specs=(WHOLE, WHOLE),
        scratch_shapes=[
            pltpu.VMEM((total, 256), BF),
            pltpu.VMEM((total, 256), BF),
            pltpu.VMEM((total, 128), BF),
            pltpu.VMEM((128, total), BF),
            pltpu.VMEM((128, total), BF),
            pltpu.VMEM((total, 128), F32),
            pltpu.VMEM((total, 128), F32),
            pltpu.VMEM((2, total, total // 8), F32),
            pltpu.VMEM((2, total, total // 8), F32),
            pltpu.VMEM((2, total, total // 8), BF),
        ],
    )(pos, *parts, dout, ids)


def chosen_rows(dp, source, half, target):
    for r in range(8):
        for s in range(8):
            rows = pl.ds(pl.multiple_of(s * 128 + (dp ^ (2 * r + half)) * 8, 8), 8)
            target[r * 64 + s * 8 : r * 64 + s * 8 + 8, :] = source[rows, :]


def projection_kernel(places, pos, get, gain, keep, send, own_gain, grad, other, sums):
    dqkv, weights = get(0), get(1)
    rows = dqkv.shape[0] // 8
    total = None
    for i, (r, offset) in enumerate(places):
        normed = get(2 + i)
        size = normed.shape[0]
        rng = pl.ds(pl.multiple_of((pos[0] ^ r) * rows + offset, size), size)
        term = mm(dqkv[rng, :], normed[...], 0, 0)
        total = term if total is None else total + term
    grad[...] = total.T
    weighted = jnp.sum(total * weights[...].T.astype(F32), axis=0, keepdims=True) / gain[...]
    sums[...] = jnp.zeros_like(sums)
    for j in range(8):
        sums[j : j + 1, :] = weighted[:, j * 128 : (j + 1) * 128]
    high = sums[...].astype(BF)
    low = (sums[...] - high.astype(F32)).astype(BF)
    own_gain[...] = (high.astype(F32) + low.astype(F32))[:8, :]
    chosen_rows(pos[1], grad, 0, keep)
    chosen_rows(pos[1], grad, 1, other)
    send[:512, :] = other[...].astype(BF)
    send[512:, :128] = high
    send[512:, 128:256] = low
    send[512:, 256:] = jnp.zeros_like(low)


def side_by_side(source, target):
    for h in range(HEADS):
        target[:, h * 128 : (h + 1) * 128] = source[h]


def output_gradient_kernel(
    pos, get, own_gain, send_near, send_far, keep, middle, gain_sum, grad, chosen, flat, twin, sums
):
    side_by_side(get(0), flat)
    own = mm(flat[...], get(1)[...], 0, 0)
    side_by_side(get(2), twin)
    grad[...] = own + mm(twin[...], get(3)[...], 0, 0)
    chosen_rows(pos[1], grad, 0, chosen)
    arrived = get(5)[...].astype(F32)
    qkv = get(4)[...] + arrived[:512, :]
    left, right = slice(0, 640), slice(640, 1408)
    first, second = qkv[:, :128], qkv[:, 128:]
    send_near[:256, :128] = first[128:384].astype(BF)
    send_near[:256, 128:] = chosen[128:384, :512].astype(BF)
    send_far[:, :256] = second[256:].astype(BF)
    send_far[:, 256:] = chosen[256:, 512:].astype(BF)
    for target, near_rows, far_rows in (
        (keep, slice(0, 128), slice(0, 128)),
        (middle, slice(384, 512), slice(128, 256)),
    ):
        target[:, left] = jnp.concatenate([first[near_rows], chosen[near_rows, :512]], axis=1)
        target[:, right] = jnp.concatenate([second[far_rows], chosen[far_rows, 512:]], axis=1)
    sums[...] = jnp.zeros_like(sums)
    sums[:8, :] = own_gain[...] + arrived[512:520, :128] + arrived[512:520, 128:256]
    high = sums[...].astype(BF)
    low = (sums[...] - high.astype(F32)).astype(BF)
    gain_sum[...] = (high.astype(F32) + low.astype(F32))[:8, :]
    send_near[256:, :128] = high
    send_near[256:, 128:256] = low
    send_near[256:, 256:] = jnp.zeros((16, 384), BF)


def layer_out_kernel(get, layer_out, flat):
    side_by_side(get(1), flat)
    layer_out[...] = (get(0)[...].astype(F32) + mm(flat[...], get(2)[...], 1, 0)).astype(BF)


def frame_gradient_kernel(get, gain, w_qkv, result, weights, flat, semaphores):
    width = get(0).shape[1]
    copies = []
    for t in range(3):
        part = w_qkv.at[:, t * width : (t + 1) * width]
        copies.append(pltpu.make_async_copy(part, weights.at[t], semaphores.at[t]))
    for copy in copies:
        copy.start()
    xhat, rstd = layernorm(get(0)[...].astype(F32))
    total = None
    for t in range(3):
        for h in range(HEADS):
            flat[t, :, h * 128 : (h + 1) * 128] = get(1)[h][:, t * 128 : (t + 1) * 128]
        copies[t].wait()
        term = mm(weights[t], flat[t], 1, 1)
        total = term if total is None else total + term
    g = total.T * gain[...]
    mean_g = jnp.mean(g, axis=-1, keepdims=True)
    mean_gx = jnp.mean(g * xhat, axis=-1, keepdims=True)
    result[...] = (get(2)[...].astype(F32) + rstd * (g - mean_g - xhat * mean_gx)).astype(BF)


def high_low(x):
    high = lax.reduce_precision(x, 8, 7)
    low = lax.reduce_precision(x - high, 8, 7)
    return high, low


def packed(x, columns):
    high, low = high_low(x)
    both = jnp.concatenate([high, low], axis=1).astype(BF)
    return jnp.pad(both, ((0, 0), (0, columns - 256)))


def unpacked(x):
    return x[:, :128].astype(F32) + x[:, 128:256].astype(F32)


def settled(x):
    high, low = high_low(x)
    return high + low


def on_device(frames, layernorm_gain, w_qkv, w_out, segment_ids, output_gradient):
    x = frames[0]
    grad_out = output_gradient[0]
    rows, width = x.shape
    head = width // HEADS
    scale = head**-0.5
    pos = jnp.stack([lax.axis_index("seq"), lax.axis_index("dp")]).astype(jnp.int32)
    gain_row = layernorm_gain[None, :]

    own = call(
        layernorm_kernel, "layernorm", shape(BF, rows, width), in_specs=[WHOLE] * 2, out_specs=WHOLE
    )(x, gain_row)
    grad_twin = dp_swap(grad_out, 1)
    beside = seq_swap(own, 1)
    after, before = seq_swap(own, 2), seq_swap(own, 6)
    half = rows // 2
    far = [seq_swap(after[:half], 6), seq_swap(before[half:], 2)]
    beyond = [seq_swap(part, 1) for part in far]
    normed = {
        (0, 0): own,
        (1, 0): beside,
        (2, 0): after,
        (6, 0): before,
        (3, 0): seq_swap(beside, 2),
        (7, 0): seq_swap(beside, 6),
        (4, 0): far[0],
        (4, half): far[1],
        (5, 0): beyond[0],
        (5, half): beyond[1],
    }
    places, normed = list(normed), list(normed.values())

    dattn, w_head = staged(
        dattn_kernel,
        "dattn",
        [shape(BF, HEADS, rows, head), shape(BF, width, 384)],
        [pos],
        [grad_out, w_out],
        left=[w_qkv],
        scratch=[pltpu.SemaphoreType.DMA((3,))],
    )
    parts = [mm(n, w_head, 1, 0).astype(BF) for n in normed]
    dattn, grad_twin, _ = lax.optimization_barrier((dattn, grad_twin, beyond[1]))
    dout = seq_exchange(dattn)

    attn_head, dqkv_head = attention(pos, parts, places, dout, segment_ids, scale)
    attn = seq_exchange(attn_head.reshape(8, rows, head))
    dqkv = seq_exchange(dqkv_head.reshape(8, rows, 384))
    wqkv_keep, wqkv_send, gain_part = staged(
        functools.partial(projection_kernel, places),
        "projection_gradient",
        [shape(F32, 512, 384), shape(BF, 528, 384), shape(F32, 8, 128)],
        [pos],
        [dqkv_head, w_head] + normed,
        [gain_row],
        scratch=[
            pltpu.VMEM((1024, 384), F32),
            pltpu.VMEM((512, 384), F32),
            pltpu.VMEM((16, 128), F32),
        ],
    )
    attn, wqkv_send, gain_part = lax.optimization_barrier((attn, wqkv_send, gain_part))
    attn_twin = dp_swap(attn, 1)
    got = dp_swap(wqkv_send, 1)
    near, away, keep, middle, gain_sum = staged(
        output_gradient_kernel,
        "output_gradient",
        [shape(BF, 272, 640), shape(BF, 256, 768)]
        + [shape(F32, 128, 1408)] * 2
        + [shape(F32, 8, 128)],
        [pos],
        [attn, grad_out, attn_twin, grad_twin, wqkv_keep, got],
        [gain_part],
        scratch=[
            pltpu.VMEM((1024, 1024), F32),
            pltpu.VMEM((512, 1024), F32),
            pltpu.VMEM((rows, width), BF),
            pltpu.VMEM((rows, width), BF),
            pltpu.VMEM((16, 128), F32),
        ],
        vmem=40 * 1024 * 1024,
    )
    near, away = dp_swap(near, 4), dp_swap(away, 12)
    (layer_out,) = staged(
        layer_out_kernel,
        "layer_out",
        [shape(BF, rows, width)],
        [],
        [x, attn, w_out],
        scratch=[pltpu.VMEM((rows, width), BF)],
    )
    near, away, layer_out = lax.optimization_barrier((near, away, layer_out))
    gain_sum = gain_sum + unpacked(near[256:264])
    near_next = (middle[:, :640] + near[128:256].astype(F32)).astype(BF)
    near_next = dp_swap(jnp.concatenate([near_next, packed(gain_sum, 640)], axis=0), 12)
    away_next = dp_swap((middle[:, 640:] + away[:128].astype(F32)).astype(BF), 4)
    gain_sum = settled(gain_sum) + unpacked(near_next[128:])
    sums = keep + jnp.concatenate(
        [
            near[:128].astype(F32) + near_next[:128].astype(F32),
            away[128:].astype(F32) + away_next.astype(F32),
        ],
        axis=1,
    )
    got = dp_swap(jnp.concatenate([sums[64:].astype(BF), packed(gain_sum, 1408)], axis=0), 2)
    gain_sum = settled(gain_sum) + unpacked(got[64:])
    sums = sums[:64] + got[:64].astype(F32)
    sums = jnp.concatenate(
        [sums[:, :128], sums[:, 640:896], sums[:, 128:640], sums[:, 896:]], axis=1
    )
    sums, dqkv = lax.optimization_barrier((sums, dqkv))
    (frame_grad,) = staged(
        frame_gradient_kernel,
        "frame_gradient",
        [shape(BF, rows, width)],
        [],
        [x, dqkv, grad_out],
        [gain_row],
        [w_qkv],
        [
            pltpu.VMEM((3, width, width), BF),
            pltpu.VMEM((3, rows, width), BF),
            pltpu.SemaphoreType.DMA((3,)),
        ],
    )

    note = jnp.broadcast_to(packed(gain_sum, 256)[None], (8, 8, 256))
    got = seq_exchange(jnp.concatenate([sums.reshape(8, 8, 1408).astype(BF), note], axis=2))
    grad_wqkv = got[:, :, :384].reshape(8, 8, 3, head).transpose(1, 2, 0, 3).reshape(8, 3 * width)
    grad_wout = jnp.sum(got[:, :, 384:1408].astype(F32), axis=0).astype(BF)
    totals = [unpacked(got[s, :, 1408:]) for s in range(8)]
    grad_gain = functools.reduce(lambda a, b: a + b, totals).reshape(width)
    return (
        layer_out[None],
        frame_grad[None],
        grad_wqkv,
        grad_wout,
        grad_gain,
    )


def solution(mesh):
    placed = (P("dp", "seq", None), P(), P(), P(), P("dp", None), P("dp", "seq", None))
    return jax.shard_map(
        on_device,
        mesh=mesh,
        in_specs=placed,
        out_specs=(
            P("dp", "seq", None),
            P("dp", "seq", None),
            P(("seq", "dp"), None),
            P(("seq", "dp"), None),
            P(),
        ),
        check_vma=False,
    )
```

profile of v0, /device:TPU:0, one launch (start us, length us, event | category | flops | bytes accessed | tf_op | source)
XLA Modules:
  0.0 137.9 jit_solution(9119790028021093822)
XLA Ops:
  0.6 2.2 %layernorm.1.refs_3_ = bf16[256,1024]{1,0:T(8,128)(2,1)} custom-call(bf16[256,1024]{1,0:T(8,128)(2,1)} %bitcast.59, f32[1,1024]{1,0:T(1,128)} %bitcast.66), custom_call_target="tpu_custom_call" | custom-call | tf_op jit(solution)/shard_map/layernorm/pallas_call | solution.py:343
  2.8 3.1 %collective-permute-start.2 = (bf16[256,1024]{1,0:T(8,128)(2,1)}, bf16[256,1024]{1,0:T(8,128)(2,1)S(1)}, u32[]{:S(2)}, u32[]{:S(2)}) collective-permute-start(bf16[256,1024]{1,0:T(8,128)(2,1)} %layernorm.1.refs_3_), channel_id=1, source_target_pairs={{0,96},{16,112},{32,64},{48,80},{64,32},{80,48},{96,0},{112,16},{1... | collective-permute-start | bytes 1572872 | tf_op jit(solution)/shard_map/ppermute | solution.py:22
  5.9 0.1 collective-permute-start.1
  6.1 1.9 %collective-permute-start = (bf16[256,1024]{1,0:T(8,128)(2,1)}, bf16[256,1024]{1,0:T(8,128)(2,1)}, u32[]{:S(2)}, u32[]{:S(2)}) collective-permute-start(bf16[256,1024]{1,0:T(8,128)(2,1)} %layernorm.1.refs_3_), channel_id=1, source_target_pairs={{0,16},{16,0},{32,48},{48,32},{64,80},{80,64},{96,112},{112,96},{1... | collective-permute-start | bytes 1572872 | tf_op jit(solution)/shard_map/ppermute | solution.py:22
  8.0 0.0 collective-permute-start.9
  8.0 0.6 pad_add_fusion.refs_0_.pos
  8.6 4.6 %dattn.1 = (bf16[8,256,128]{2,1,0:T(8,128)(2,1)}, bf16[1024,384]{1,0:T(8,128)(2,1)}) custom-call(s32[2]{0:T(128)} %pad_add_fusion.refs_0_.pos, bf16[256,1024]{1,0:T(8,128)(2,1)} %bitcast.56, bf16[1024,1024]{1,0:T(8,128)(2,1)} %refs_2_.3, bf16[1024,3072]{1,0:T(8,128)(2,1)} %refs_4_.1), custom_call_target="tpu_custom_call" | custom-call | tf_op jit(solution)/shard_map/dattn/pallas_call | solution.py:84
  13.2 1.6 %convolution_convert_fusion.5.refs_0_ = bf16[256,384]{1,0:T(8,128)(2,1)S(1)} fusion(bf16[256,1024]{1,0:T(8,128)(2,1)S(1)} %copy-done.8, bf16[1024,384]{1,0:T(8,128)(2,1)} %get-tuple-element.27.refs_2_), kind=kOutput, calls=%fused_computation.5 | convolution fusion | flops 201424896 | bytes 1507328 | tf_op jit(solution)/shard_map/dot_general | solution.py:34
  14.8 3.2 %collective-permute-done.2.refs_6_ = bf16[256,1024]{1,0:T(8,128)(2,1)S(1)} collective-permute-done((bf16[256,1024]{1,0:T(8,128)(2,1)}, bf16[256,1024]{1,0:T(8,128)(2,1)S(1)}, u32[]{:S(2)}, u32[]{:S(2)}) %collective-permute-start.2) | collective-permute-done | bytes 524320 | tf_op jit(solution)/shard_map/ppermute | solution.py:22
  18.1 0.4 collective-permute-start.6
  18.5 1.1 collective-permute-done.1.refs_5_
  19.5 1.7 %collective-permute-start.5 = (bf16[128,1024]{1,0:T(8,128)(2,1)S(1)}, bf16[128,1024]{1,0:T(8,128)(2,1)S(1)}, u32[]{:S(2)}, u32[]{:S(2)}) collective-permute-start(bf16[128,1024]{1,0:T(8,128)(2,1)S(1)} %slice.202), channel_id=1, source_target_pairs={{0,96},{16,112},{32,64},{48,80},{64,32},{80,48},{96,0},{112,16},{1... | collective-permute-start | bytes 786440 | tf_op jit(solution)/shard_map/ppermute | solution.py:22
  21.3 1.6 %collective-permute-start.4 = (bf16[256,1024]{1,0:T(8,128)(2,1)}, bf16[256,1024]{1,0:T(8,128)(2,1)}, u32[]{:S(2)}, u32[]{:S(2)}) collective-permute-start(bf16[256,1024]{1,0:T(8,128)(2,1)} %collective-permute-done.refs_4_), channel_id=1, source_target_pairs={{0,96},{16,112},{32,64},{48,80},{64,32},{80,48},{96,0},{112,16},{1... | collective-permute-start | bytes 1572872 | tf_op jit(solution)/shard_map/ppermute | solution.py:22
  22.9 0.4 convolution_convert_fusion.2.refs_3_
  23.3 0.4 convolution_convert_fusion.3.refs_2_
  23.8 1.5 %convolution_convert_fusion.4.refs_1_ = bf16[256,384]{1,0:T(8,128)(2,1)S(1)} fusion(bf16[256,1024]{1,0:T(8,128)(2,1)} %collective-permute-done.refs_4_, bf16[1024,384]{1,0:T(8,128)(2,1)S(1)} %copy-done.7), kind=kOutput, calls=%fused_computation.4 | convolution fusion | flops 201424896 | bytes 1507328 | tf_op jit(solution)/shard_map/dot_general | solution.py:34
  25.2 1.8 %collective-permute-done.6.refs_10_ = bf16[128,1024]{1,0:T(8,128)(2,1)S(1)} collective-permute-done((bf16[128,1024]{1,0:T(8,128)(2,1)S(1)}, bf16[128,1024]{1,0:T(8,128)(2,1)S(1)}, u32[]{:S(2)}, u32[]{:S(2)}) %collective-permute-start.6) | collective-permute-done | bytes 262176 | tf_op jit(solution)/shard_map/ppermute | solution.py:22
  27.1 1.7 %collective-permute-start.8 = (bf16[128,1024]{1,0:T(8,128)(2,1)S(1)}, bf16[128,1024]{1,0:T(8,128)(2,1)S(1)}, u32[]{:S(2)}, u32[]{:S(2)}) collective-permute-start(bf16[128,1024]{1,0:T(8,128)(2,1)S(1)} %collective-permute-done.6.refs_10_), channel_id=1, source_target_pairs={{0,16},{16,0},{32,48},{48,32},{64,80},{80,64},{96,112},{112,96},{1... | collective-permute-start | bytes 786440 | tf_op jit(solution)/shard_map/ppermute | solution.py:22
  28.8 0.3 convolution_convert_fusion.8.refs_7_
  29.1 0.9 collective-permute-done.5.refs_9_
  30.1 1.9 %collective-permute-start.7 = (bf16[128,1024]{1,0:T(8,128)(2,1)S(1)}, bf16[128,1024]{1,0:T(8,128)(2,1)}, u32[]{:S(2)}, u32[]{:S(2)}) collective-permute-start(bf16[128,1024]{1,0:T(8,128)(2,1)S(1)} %collective-permute-done.5.refs_9_), channel_id=1, source_target_pairs={{0,16},{16,0},{32,48},{48,32},{64,80},{80,64},{96,112},{112,96},{1... | collective-permute-start | bytes 786440 | tf_op jit(solution)/shard_map/ppermute | solution.py:22
  32.0 0.3 convolution_convert_fusion.9.refs_6_
  32.3 0.0 collective-permute-done.9.refs_4_
  32.3 2.4 %collective-permute-done.8.refs_12_ = bf16[128,1024]{1,0:T(8,128)(2,1)S(1)} collective-permute-done((bf16[128,1024]{1,0:T(8,128)(2,1)S(1)}, bf16[128,1024]{1,0:T(8,128)(2,1)S(1)}, u32[]{:S(2)}, u32[]{:S(2)}) %collective-permute-start.8) | collective-permute-done | bytes 262176 | tf_op jit(solution)/shard_map/ppermute | solution.py:22
  34.7 5.5 %all-to-all-start = ((bf16[8,256,128]{2,1,0:T(8,128)(2,1)}), bf16[8,256,128]{2,1,0:T(8,128)(2,1)S(1)}, u32[]{:S(2)}, u32[]{:S(2)}) async-start(bf16[8,256,128]{2,1,0:T(8,128)(2,1)} %get-tuple-element.29), calls=%async_computation | async-start | bytes 1048576 | tf_op jit(solution)/shard_map/all_to_all | solution.py:30
  40.2 0.3 convolution_convert_fusion.6.refs_9_
  40.5 0.0 copy-start.3
  40.5 0.0 copy-start.4
  40.6 1.5 %convolution_convert_fusion.refs_5_ = bf16[256,384]{1,0:T(8,128)(2,1)S(1)} fusion(bf16[256,1024]{1,0:T(8,128)(2,1)} %collective-permute-done.4.refs_8_, bf16[1024,384]{1,0:T(8,128)(2,1)S(1)} %copy-done.7), kind=kOutput, calls=%fused_computation | convolution fusion | flops 201424896 | bytes 1507328 | tf_op jit(solution)/shard_map/dot_general | solution.py:34
  42.0 0.0 collective-permute-done.7.refs_11_
  42.0 1.2 convolution_convert_fusion.7.refs_8_
  43.3 1.5 %convolution_convert_fusion.1.refs_4_ = bf16[256,384]{1,0:T(8,128)(2,1)S(1)} fusion(bf16[256,1024]{1,0:T(8,128)(2,1)} %collective-permute-done.3.refs_7_, bf16[1024,384]{1,0:T(8,128)(2,1)S(1)} %copy-done.7), kind=kOutput, calls=%fused_computation.1 | convolution fusion | flops 201424896 | bytes 1507328 | tf_op jit(solution)/shard_map/dot_general | solution.py:34
  44.8 3.6 %all-to-all-done.refs_10_ = bf16[8,256,128]{2,1,0:T(8,128)(2,1)S(1)} async-done(((bf16[8,256,128]{2,1,0:T(8,128)(2,1)}), bf16[8,256,128]{2,1,0:T(8,128)(2,1)S(1)}, u32[]{:S(2)}, u32[]{:S(2)}) %all-to-all-start) | async-done | bytes 524320 | tf_op jit(solution)/shard_map/all_to_all | solution.py:30
  48.4 20.5 %attention.1 = (bf16[2048,128]{1,0:T(8,128)(2,1)}, bf16[2048,384]{1,0:T(8,128)(2,1)}) custom-call(s32[2]{0:T(128)S(1)} %copy-done.4, bf16[256,384]{1,0:T(8,128)(2,1)S(1)} %convolution_convert_fusion.5.refs_0_, bf16[256,384]{1,0:T(8,128)(2,1)S(1)} %convolution_convert_fusion.4.refs_1_, bf16[256,384]{1,0:T(8,128)(2,1)S(1)} %convolution_convert_fusion.3.refs_2_, ...), custom_call_target="tpu_custom_call" | custom-call | tf_op jit(solution)/shard_map/attention/pallas_call | solution.py:194
  68.8 3.7 %all-to-all-start.1 = ((bf16[8,256,128]{2,1,0:T(8,128)(2,1)}), bf16[8,256,128]{2,1,0:T(8,128)(2,1)S(1)}, u32[]{:S(2)}, u32[]{:S(2)}) async-start(bf16[8,256,128]{2,1,0:T(8,128)(2,1)} %bitcast.5), calls=%async_computation.1 | async-start | bytes 1048576 | tf_op jit(solution)/shard_map/all_to_all | solution.py:30
  72.6 0.0 copy-start
  72.6 0.0 copy-start.5
  72.6 7.1 %projection_gradient.1 = (f32[512,384]{1,0:T(8,128)}, bf16[528,384]{1,0:T(8,128)(2,1)}, f32[8,128]{1,0:T(8,128)}) custom-call(s32[2]{0:T(128)} %pad_add_fusion.refs_0_.pos, bf16[2048,384]{1,0:T(8,128)(2,1)} %get-tuple-element.31.refs_1_, bf16[1024,384]{1,0:T(8,128)(2,1)} %get-tuple-element.27.refs_2_, bf16[256,1024]{1,0:T(8,128)(2,1)} %layernorm.1.refs_3_, ...), custom_call_target="tpu_custom_call" | custom-call | tf_op jit(solution)/shard_map/projection_gradient/pallas_call | solution.py:84
  79.7 0.7 all-to-all-done.1.refs_1_
  80.4 0.0 collective-permute-start.10
  80.4 0.5 collective-permute-start.11
  81.0 2.1 %collective-permute-done.11.refs_6_ = bf16[528,384]{1,0:T(8,128)(2,1)S(1)} collective-permute-done((bf16[528,384]{1,0:T(8,128)(2,1)}, bf16[528,384]{1,0:T(8,128)(2,1)S(1)}, u32[]{:S(2)}, u32[]{:S(2)}) %collective-permute-start.11) | collective-permute-done | bytes 405536 | tf_op jit(solution)/shard_map/ppermute | solution.py:26
  83.0 1.1 copy-done.2
  84.2 0.7 copy-done.6
  84.8 3.7 %output_gradient.1 = (bf16[272,640]{1,0:T(8,128)(2,1)}, bf16[256,768]{1,0:T(8,128)(2,1)S(1)}, f32[128,1408]{1,0:T(8,128)S(1)}, f32[128,1408]{1,0:T(8,128)S(1)}, f32[8,128]{1,0:T(8,128)S(1)}) custom-call(s32[2]{0:T(128)S(1)} %copy-done.5, bf16[8,256,128]{2,1,0:T(8,128)(2,1)S(1)} %all-to-all-done.1.refs_1_, bf16[256,1024]{1,0:T(8,128)(2,1)S(1)} %bitcast.58, ...), custom_call_target="tpu_custom_call" | custom-call | tf_op jit(solution)/shard_map/output_gradient/pallas_call | solution.py:84
  88.6 2.8 %collective-permute-start.13 = (bf16[256,768]{1,0:T(8,128)(2,1)S(1)}, bf16[256,768]{1,0:T(8,128)(2,1)S(1)}, u32[]{:S(2)}, u32[]{:S(2)}) collective-permute-start(bf16[256,768]{1,0:T(8,128)(2,1)S(1)} %get-tuple-element.40), channel_id=1, source_target_pairs={{0,12},{1,13},{2,14},{3,15},{4,8},{5,9},{6,10},{7,11},{8,4},{9,5},... | collective-permute-start | bytes 1179656 | tf_op jit(solution)/shard_map/ppermute | solution.py:26
  91.4 0.2 collective-permute-start.12
  91.6 4.9 %all-to-all-start.2 = ((bf16[8,256,384]{2,1,0:T(8,128)(2,1)}), bf16[8,256,384]{2,1,0:T(8,128)(2,1)}, u32[]{:S(2)}, u32[]{:S(2)}) async-start(bf16[8,256,384]{2,1,0:T(8,128)(2,1)} %bitcast.7), calls=%async_computation.2 | async-start | bytes 3145728 | tf_op jit(solution)/shard_map/all_to_all | solution.py:30
  96.5 3.5 %layer_out.1 = bf16[256,1024]{1,0:T(8,128)(2,1)} custom-call(bf16[256,1024]{1,0:T(8,128)(2,1)} %bitcast.60, bf16[8,256,128]{2,1,0:T(8,128)(2,1)} %copy-done.1, bf16[1024,1024]{1,0:T(8,128)(2,1)} %refs_2_.3), custom_call_target="tpu_custom_call" | custom-call | tf_op jit(solution)/shard_map/layer_out/pallas_call | solution.py:84
  100.0 1.5 %collective-permute-done.12 = bf16[272,640]{1,0:T(8,128)(2,1)S(1)} collective-permute-done((bf16[272,640]{1,0:T(8,128)(2,1)}, bf16[272,640]{1,0:T(8,128)(2,1)S(1)}, u32[]{:S(2)}, u32[]{:S(2)}) %collective-permute-start.12) | collective-permute-done | bytes 348192 | tf_op jit(solution)/shard_map/ppermute | solution.py:26
  101.6 2.3 %collective-permute-start.14 = (bf16[136,640]{1,0:T(8,128)(2,1)S(1)}, bf16[136,640]{1,0:T(8,128)(2,1)S(1)}, u32[]{:S(2)}, u32[]{:S(2)}) collective-permute-start(bf16[136,640]{1,0:T(8,128)(2,1)S(1)} %pad_maximum_fusion.3), channel_id=1, source_target_pairs={{0,12},{1,13},{2,14},{3,15},{4,8},{5,9},{6,10},{7,11},{8,4},{9,5},... | collective-permute-start | bytes 522248 | tf_op jit(solution)/shard_map/ppermute | solution.py:26
  104.0 0.1 collective-permute-start.15
  104.1 4.3 %collective-permute-done.14 = bf16[136,640]{1,0:T(8,128)(2,1)S(1)} collective-permute-done((bf16[136,640]{1,0:T(8,128)(2,1)S(1)}, bf16[136,640]{1,0:T(8,128)(2,1)S(1)}, u32[]{:S(2)}, u32[]{:S(2)}) %collective-permute-start.14) | collective-permute-done | bytes 174112 | tf_op jit(solution)/shard_map/ppermute | solution.py:26
  108.4 1.5 %collective-permute-done.15 = bf16[128,768]{1,0:T(8,128)(2,1)S(1)} collective-permute-done((bf16[128,768]{1,0:T(8,128)(2,1)S(1)}, bf16[128,768]{1,0:T(8,128)(2,1)S(1)}, u32[]{:S(2)}, u32[]{:S(2)}) %collective-permute-start.15) | collective-permute-done | bytes 196640 | tf_op jit(solution)/shard_map/ppermute | solution.py:26
  109.9 0.1 maximum_add_fusion
  110.1 3.7 %collective-permute-start.16 = (bf16[72,1408]{1,0:T(8,128)(2,1)S(1)}, bf16[72,1408]{1,0:T(8,128)(2,1)S(1)}, u32[]{:S(2)}, u32[]{:S(2)}) collective-permute-start(bf16[72,1408]{1,0:T(8,128)(2,1)S(1)} %pad_maximum_fusion.2), channel_id=1, source_target_pairs={{0,2},{1,3},{2,0},{3,1},{4,6},{5,7},{6,4},{7,5},{8,10},{9,11},{10,... | collective-permute-start | bytes 608264 | tf_op jit(solution)/shard_map/ppermute | solution.py:26
  113.7 8.0 %collective-permute-done.16 = bf16[72,1408]{1,0:T(8,128)(2,1)S(1)} collective-permute-done((bf16[72,1408]{1,0:T(8,128)(2,1)S(1)}, bf16[72,1408]{1,0:T(8,128)(2,1)S(1)}, u32[]{:S(2)}, u32[]{:S(2)}) %collective-permute-start.16) | collective-permute-done | bytes 202784 | tf_op jit(solution)/shard_map/ppermute | solution.py:26
  121.9 0.7 pad_maximum_fusion.1
  122.6 4.8 %all-to-all-start.3 = ((bf16[8,8,1664]{2,1,0:T(8,128)(2,1)}), bf16[8,8,1664]{2,1,0:T(8,128)(2,1)S(1)}, u32[]{:S(2)}, u32[]{:S(2)}) async-start(bf16[8,8,1664]{2,1,0:T(8,128)(2,1)} %pad_maximum_fusion.1), calls=%async_computation.3 | async-start | bytes 425984 | tf_op jit(solution)/shard_map/all_to_all | solution.py:30
  127.4 8.7 %frame_gradient.1 = bf16[256,1024]{1,0:T(8,128)(2,1)} custom-call(bf16[256,1024]{1,0:T(8,128)(2,1)} %bitcast.61, bf16[8,256,384]{2,1,0:T(8,128)(2,1)} %all-to-all-done.2.refs_1_, bf16[256,1024]{1,0:T(8,128)(2,1)} %bitcast.57, f32[1,1024]{1,0:T(1,128)} %bitcast.68, bf16[1024,3072]{1,0:T(8,128)(2,1)} %refs_4_.1), custom_call_target="tpu_custom_call" | custom-call | tf_op jit(solution)/shard_map/frame_gradient/pallas_call | solution.py:84
  136.0 0.0 all-to-all-done.3
  136.1 0.6 copy.11
  136.7 0.6 add_bitcast_fusion
  137.3 0.6 slice_reduce_fusion
  (53 shorter events, 0.5 us)
Async XLA Ops:
  2.8 15.2 %collective-permute-start.2 = (bf16[256,1024]{1,0:T(8,128)(2,1)}, bf16[256,1024]{1,0:T(8,128)(2,1)S(1)}, u32[]{:S(2)}, u32[]{:S(2)}) collective-permute-start(bf16[256,1024]{1,0:T(8,128)(2,1)} %layernorm.1.refs_3_), channel_id=1, source_target_pairs={{0,96},{16,112},{32,64},{48,80},{64,32},{80,48},{96,0},{112,16},{1... | collective-permute-start | bytes 1572872 | tf_op jit(solution)/shard_map/ppermute | solution.py:22
  5.9 13.6 %collective-permute-start.1 = (bf16[256,1024]{1,0:T(8,128)(2,1)}, bf16[256,1024]{1,0:T(8,128)(2,1)S(1)}, u32[]{:S(2)}, u32[]{:S(2)}) collective-permute-start(bf16[256,1024]{1,0:T(8,128)(2,1)} %layernorm.1.refs_3_), channel_id=1, source_target_pairs={{0,32},{16,48},{32,0},{48,16},{64,96},{80,112},{96,64},{112,80},{1... | collective-permute-start | bytes 1572872 | tf_op jit(solution)/shard_map/ppermute | solution.py:22
  6.1 15.2 %collective-permute-start = (bf16[256,1024]{1,0:T(8,128)(2,1)}, bf16[256,1024]{1,0:T(8,128)(2,1)}, u32[]{:S(2)}, u32[]{:S(2)}) collective-permute-start(bf16[256,1024]{1,0:T(8,128)(2,1)} %layernorm.1.refs_3_), channel_id=1, source_target_pairs={{0,16},{16,0},{32,48},{48,32},{64,80},{80,64},{96,112},{112,96},{1... | collective-permute-start | bytes 1572872 | tf_op jit(solution)/shard_map/ppermute | solution.py:22
  8.0 24.3 %collective-permute-start.9 = (bf16[256,1024]{1,0:T(8,128)(2,1)}, bf16[256,1024]{1,0:T(8,128)(2,1)S(1)}, u32[]{:S(2)}, u32[]{:S(2)}) collective-permute-start(bf16[256,1024]{1,0:T(8,128)(2,1)} %bitcast.55), channel_id=1, source_target_pairs={{0,1},{1,0},{2,3},{3,2},{4,5},{5,4},{6,7},{7,6},{8,9},{9,8},{10,11... | collective-permute-start | bytes 1572872 | tf_op jit(solution)/shard_map/ppermute | solution.py:26
  8.6 4.6 %copy-start.8 = (bf16[256,1024]{1,0:T(8,128)(2,1)S(1)}, bf16[256,1024]{1,0:T(8,128)(2,1)}, u32[]{:S(2)}) copy-start(bf16[256,1024]{1,0:T(8,128)(2,1)} %layernorm.1.refs_3_) | copy-start | bytes 1572868
  13.2 9.7 %copy-start.7 = (bf16[1024,384]{1,0:T(8,128)(2,1)S(1)}, bf16[1024,384]{1,0:T(8,128)(2,1)}, u32[]{:S(2)}) copy-start(bf16[1024,384]{1,0:T(8,128)(2,1)} %get-tuple-element.27.refs_2_) | copy-start | bytes 2359300
  18.1 4.8 %copy-start.9 = (bf16[256,1024]{1,0:T(8,128)(2,1)}, bf16[256,1024]{1,0:T(8,128)(2,1)S(1)}, u32[]{:S(2)}) copy-start(bf16[256,1024]{1,0:T(8,128)(2,1)S(1)} %collective-permute-done.2.refs_6_) | copy-start | bytes 1572868
  18.1 9.0 %collective-permute-start.6 = (bf16[128,1024]{1,0:T(8,128)(2,1)S(1)}, bf16[128,1024]{1,0:T(8,128)(2,1)S(1)}, u32[]{:S(2)}, u32[]{:S(2)}) collective-permute-start(bf16[128,1024]{1,0:T(8,128)(2,1)S(1)} %slice.203), channel_id=1, source_target_pairs={{0,32},{16,48},{32,0},{48,16},{64,96},{80,112},{96,64},{112,80},{1... | collective-permute-start | bytes 786440 | tf_op jit(solution)/shard_map/ppermute | solution.py:22
  19.5 5.7 %copy-start.10 = (bf16[256,1024]{1,0:T(8,128)(2,1)}, bf16[256,1024]{1,0:T(8,128)(2,1)S(1)}, u32[]{:S(2)}) copy-start(bf16[256,1024]{1,0:T(8,128)(2,1)S(1)} %collective-permute-done.1.refs_5_) | copy-start | bytes 1572868
  19.5 10.5 %collective-permute-start.5 = (bf16[128,1024]{1,0:T(8,128)(2,1)S(1)}, bf16[128,1024]{1,0:T(8,128)(2,1)S(1)}, u32[]{:S(2)}, u32[]{:S(2)}) collective-permute-start(bf16[128,1024]{1,0:T(8,128)(2,1)S(1)} %slice.202), channel_id=1, source_target_pairs={{0,96},{16,112},{32,64},{48,80},{64,32},{80,48},{96,0},{112,16},{1... | collective-permute-start | bytes 786440 | tf_op jit(solution)/shard_map/ppermute | solution.py:22
  21.3 19.3 %collective-permute-start.4 = (bf16[256,1024]{1,0:T(8,128)(2,1)}, bf16[256,1024]{1,0:T(8,128)(2,1)}, u32[]{:S(2)}, u32[]{:S(2)}) collective-permute-start(bf16[256,1024]{1,0:T(8,128)(2,1)} %collective-permute-done.refs_4_), channel_id=1, source_target_pairs={{0,96},{16,112},{32,64},{48,80},{64,32},{80,48},{96,0},{112,16},{1... | collective-permute-start | bytes 1572872 | tf_op jit(solution)/shard_map/ppermute | solution.py:22
  22.9 20.4 %collective-permute-start.3 = (bf16[256,1024]{1,0:T(8,128)(2,1)}, bf16[256,1024]{1,0:T(8,128)(2,1)}, u32[]{:S(2)}, u32[]{:S(2)}) collective-permute-start(bf16[256,1024]{1,0:T(8,128)(2,1)} %collective-permute-done.refs_4_), channel_id=1, source_target_pairs={{0,32},{16,48},{32,0},{48,16},{64,96},{80,112},{96,64},{112,80},{1... | collective-permute-start | bytes 1572872 | tf_op jit(solution)/shard_map/ppermute | solution.py:22
  27.1 5.2 %copy-start.11 = (bf16[128,1024]{1,0:T(8,128)(2,1)}, bf16[128,1024]{1,0:T(8,128)(2,1)S(1)}, u32[]{:S(2)}) copy-start(bf16[128,1024]{1,0:T(8,128)(2,1)S(1)} %collective-permute-done.6.refs_10_) | copy-start | bytes 786436
  27.1 7.7 %collective-permute-start.8 = (bf16[128,1024]{1,0:T(8,128)(2,1)S(1)}, bf16[128,1024]{1,0:T(8,128)(2,1)S(1)}, u32[]{:S(2)}, u32[]{:S(2)}) collective-permute-start(bf16[128,1024]{1,0:T(8,128)(2,1)S(1)} %collective-permute-done.6.refs_10_), channel_id=1, source_target_pairs={{0,16},{16,0},{32,48},{48,32},{64,80},{80,64},{96,112},{112,96},{1... | collective-permute-start | bytes 786440 | tf_op jit(solution)/shard_map/ppermute | solution.py:22
  30.1 12.0 %copy-start.12 = (bf16[128,1024]{1,0:T(8,128)(2,1)}, bf16[128,1024]{1,0:T(8,128)(2,1)S(1)}, u32[]{:S(2)}) copy-start(bf16[128,1024]{1,0:T(8,128)(2,1)S(1)} %collective-permute-done.5.refs_9_) | copy-start | bytes 786436
  30.1 12.0 %collective-permute-start.7 = (bf16[128,1024]{1,0:T(8,128)(2,1)S(1)}, bf16[128,1024]{1,0:T(8,128)(2,1)}, u32[]{:S(2)}, u32[]{:S(2)}) collective-permute-start(bf16[128,1024]{1,0:T(8,128)(2,1)S(1)} %collective-permute-done.5.refs_9_), channel_id=1, source_target_pairs={{0,16},{16,0},{32,48},{48,32},{64,80},{80,64},{96,112},{112,96},{1... | collective-permute-start | bytes 786440 | tf_op jit(solution)/shard_map/ppermute | solution.py:22
  34.7 5.8 %copy-start.13 = (bf16[128,1024]{1,0:T(8,128)(2,1)}, bf16[128,1024]{1,0:T(8,128)(2,1)S(1)}, u32[]{:S(2)}) copy-start(bf16[128,1024]{1,0:T(8,128)(2,1)S(1)} %collective-permute-done.8.refs_12_) | copy-start | bytes 786436
  34.7 13.7 %all-to-all-start = ((bf16[8,256,128]{2,1,0:T(8,128)(2,1)}), bf16[8,256,128]{2,1,0:T(8,128)(2,1)S(1)}, u32[]{:S(2)}, u32[]{:S(2)}) async-start(bf16[8,256,128]{2,1,0:T(8,128)(2,1)} %get-tuple-element.29), calls=%async_computation | async-start | bytes 1048576 | tf_op jit(solution)/shard_map/all_to_all | solution.py:30
  40.5 7.9 %copy-start.3 = (s32[1,2048]{1,0:T(1,128)S(1)}, s32[1,2048]{1,0:T(1,128)}, u32[]{:S(2)}) copy-start(s32[1,2048]{1,0:T(1,128)} %refs_11_.1) | copy-start | bytes 24580
  40.5 7.9 %copy-start.4 = (s32[2]{0:T(128)S(1)}, s32[2]{0:T(128)}, u32[]{:S(2)}) copy-start(s32[2]{0:T(128)} %pad_add_fusion.refs_0_.pos) | copy-start | bytes 28
  68.8 11.6 %all-to-all-start.1 = ((bf16[8,256,128]{2,1,0:T(8,128)(2,1)}), bf16[8,256,128]{2,1,0:T(8,128)(2,1)S(1)}, u32[]{:S(2)}, u32[]{:S(2)}) async-start(bf16[8,256,128]{2,1,0:T(8,128)(2,1)} %bitcast.5), calls=%async_computation.1 | async-start | bytes 1048576 | tf_op jit(solution)/shard_map/all_to_all | solution.py:30
  72.6 10.4 %copy-start = (bf16[1,256,1024]{2,1,0:T(8,128)(2,1)S(1)}, bf16[1,256,1024]{2,1,0:T(8,128)(2,1)}, u32[]{:S(2)}) copy-start(bf16[1,256,1024]{2,1,0:T(8,128)(2,1)} %param.11) | copy-start | bytes 1572868
  72.6 10.4 %copy-start.5 = (s32[2]{0:T(128)S(1)}, s32[2]{0:T(128)}, u32[]{:S(2)}) copy-start(s32[2]{0:T(128)} %pad_add_fusion.refs_0_.pos) | copy-start | bytes 28
  80.4 11.2 %copy-start.1 = (bf16[8,256,128]{2,1,0:T(8,128)(2,1)}, bf16[8,256,128]{2,1,0:T(8,128)(2,1)S(1)}, u32[]{:S(2)}) copy-start(bf16[8,256,128]{2,1,0:T(8,128)(2,1)S(1)} %all-to-all-done.1.refs_1_) | copy-start | bytes 1572868
  80.4 2.6 %collective-permute-start.10 = (bf16[8,256,128]{2,1,0:T(8,128)(2,1)S(1)}, bf16[8,256,128]{2,1,0:T(8,128)(2,1)S(1)}, u32[]{:S(2)}, u32[]{:S(2)}) collective-permute-start(bf16[8,256,128]{2,1,0:T(8,128)(2,1)S(1)} %all-to-all-done.1.refs_1_), channel_id=1, source_target_pairs={{0,1},{1,0},{2,3},{3,2},{4,5},{5,4},{6,7},{7,6},{8,9},{9,8},{10,11... | collective-permute-start | bytes 1572872 | tf_op jit(solution)/shard_map/ppermute | solution.py:26
  80.4 2.6 %collective-permute-start.11 = (bf16[528,384]{1,0:T(8,128)(2,1)}, bf16[528,384]{1,0:T(8,128)(2,1)S(1)}, u32[]{:S(2)}, u32[]{:S(2)}) collective-permute-start(bf16[528,384]{1,0:T(8,128)(2,1)} %get-tuple-element.37), channel_id=1, source_target_pairs={{0,1},{1,0},{2,3},{3,2},{4,5},{5,4},{6,7},{7,6},{8,9},{9,8},{10,11... | collective-permute-start | bytes 1216520 | tf_op jit(solution)/shard_map/ppermute | solution.py:26
  83.0 1.1 copy-start.2
  84.2 0.7 copy-start.6
  88.6 13.0 %collective-permute-start.13 = (bf16[256,768]{1,0:T(8,128)(2,1)S(1)}, bf16[256,768]{1,0:T(8,128)(2,1)S(1)}, u32[]{:S(2)}, u32[]{:S(2)}) collective-permute-start(bf16[256,768]{1,0:T(8,128)(2,1)S(1)} %get-tuple-element.40), channel_id=1, source_target_pairs={{0,12},{1,13},{2,14},{3,15},{4,8},{5,9},{6,10},{7,11},{8,4},{9,5},... | collective-permute-start | bytes 1179656 | tf_op jit(solution)/shard_map/ppermute | solution.py:26
  91.4 10.1 %collective-permute-start.12 = (bf16[272,640]{1,0:T(8,128)(2,1)}, bf16[272,640]{1,0:T(8,128)(2,1)S(1)}, u32[]{:S(2)}, u32[]{:S(2)}) collective-permute-start(bf16[272,640]{1,0:T(8,128)(2,1)} %get-tuple-element.39), channel_id=1, source_target_pairs={{0,4},{1,5},{2,6},{3,7},{4,0},{5,1},{6,2},{7,3},{8,12},{9,13},{10,... | collective-permute-start | bytes 1044488 | tf_op jit(solution)/shard_map/ppermute | solution.py:26
  91.6 30.2 %all-to-all-start.2 = ((bf16[8,256,384]{2,1,0:T(8,128)(2,1)}), bf16[8,256,384]{2,1,0:T(8,128)(2,1)}, u32[]{:S(2)}, u32[]{:S(2)}) async-start(bf16[8,256,384]{2,1,0:T(8,128)(2,1)} %bitcast.7), calls=%async_computation.2 | async-start | bytes 3145728 | tf_op jit(solution)/shard_map/all_to_all | solution.py:30
  101.6 6.7 %collective-permute-start.14 = (bf16[136,640]{1,0:T(8,128)(2,1)S(1)}, bf16[136,640]{1,0:T(8,128)(2,1)S(1)}, u32[]{:S(2)}, u32[]{:S(2)}) collective-permute-start(bf16[136,640]{1,0:T(8,128)(2,1)S(1)} %pad_maximum_fusion.3), channel_id=1, source_target_pairs={{0,12},{1,13},{2,14},{3,15},{4,8},{5,9},{6,10},{7,11},{8,4},{9,5},... | collective-permute-start | bytes 522248 | tf_op jit(solution)/shard_map/ppermute | solution.py:26
  104.0 5.9 %collective-permute-start.15 = (bf16[128,768]{1,0:T(8,128)(2,1)S(1)}, bf16[128,768]{1,0:T(8,128)(2,1)S(1)}, u32[]{:S(2)}, u32[]{:S(2)}) collective-permute-start(bf16[128,768]{1,0:T(8,128)(2,1)S(1)} %add_convert_fusion), channel_id=1, source_target_pairs={{0,4},{1,5},{2,6},{3,7},{4,0},{5,1},{6,2},{7,3},{8,12},{9,13},{10,... | collective-permute-start | bytes 589832 | tf_op jit(solution)/shard_map/ppermute | solution.py:26
  110.1 11.6 %collective-permute-start.16 = (bf16[72,1408]{1,0:T(8,128)(2,1)S(1)}, bf16[72,1408]{1,0:T(8,128)(2,1)S(1)}, u32[]{:S(2)}, u32[]{:S(2)}) collective-permute-start(bf16[72,1408]{1,0:T(8,128)(2,1)S(1)} %pad_maximum_fusion.2), channel_id=1, source_target_pairs={{0,2},{1,3},{2,0},{3,1},{4,6},{5,7},{6,4},{7,5},{8,10},{9,11},{10,... | collective-permute-start | bytes 608264 | tf_op jit(solution)/shard_map/ppermute | solution.py:26
  122.6 13.5 %all-to-all-start.3 = ((bf16[8,8,1664]{2,1,0:T(8,128)(2,1)}), bf16[8,8,1664]{2,1,0:T(8,128)(2,1)S(1)}, u32[]{:S(2)}, u32[]{:S(2)}) async-start(bf16[8,8,1664]{2,1,0:T(8,128)(2,1)} %pad_maximum_fusion.1), calls=%async_computation.3 | async-start | bytes 425984 | tf_op jit(solution)/shard_map/all_to_all | solution.py:30
where the time goes:
time: 139 us; the launch traced here: 138 us
  Pallas kernels  50.2 us (36%)
  starting transfers between devices  41 us (29%)
  waiting for transfers between devices  31.1 us (22%)
  matrix products  9.08 us (7%)
  other arithmetic  2.89 us (2%)
  local copies, waits for them, and re-layouts  2.59 us (2%)
    pallas_call x5, Pallas kernels, staged(): call(kernel, name, tuple(out_shape), vmem, in_specs=[SCALARS] * n + [pl.B...  27.5 us
    pallas_call x1, Pallas kernels, attention(): call(functools.partial(attention_kernel, scale, places), 'attention', (sh...  20.5 us
    all_to_all x4, starting transfers between devices, seq_exchange(): return lax.all_to_all(x, 'seq', 0, 0, tiled=True)  18.9 us
    ppermute x8, waiting for transfers between devices, dp_swap(): return lax.ppermute(x, 'dp', [(i, i ^ bits) for i in range(16)])  17.3 us
    ppermute x9, starting transfers between devices, seq_swap(): return lax.ppermute(x, 'seq', [(i, i ^ bits) for i in range(8)])  12.5 us
    ppermute x8, starting transfers between devices, dp_swap(): return lax.ppermute(x, 'dp', [(i, i ^ bits) for i in range(16)])  9.66 us
    ppermute x9, waiting for transfers between devices, seq_swap(): return lax.ppermute(x, 'seq', [(i, i ^ bits) for i in range(8)])  9.48 us
    dot_general x10, matrix products, mm(): lax.dot_general(a, b, (((ca,), (cb,)), ((), ())), preferred_element_type=...  9.08 us
  transfers between devices with their start and end apart: 21, of which 12 were waited for; matrix products, arithmetic and copies ran while one was open for 7% of the time, Pallas kernels for 17%

commit v1 on v0

--- a/solution.py
+++ b/solution.py
@@ -252,7 +252,7 @@
 
 
 def output_gradient_kernel(
-    pos, get, own_gain, send_near, send_far, keep, middle, gain_sum, grad, chosen, flat, twin, sums
+    pos, get, send_near, send_far, keep, middle, gain_sum, grad, chosen, flat, twin, sums
 ):
     side_by_side(get(0), flat)
     own = mm(flat[...], get(1)[...], 0, 0)
@@ -274,7 +274,7 @@
         target[:, left] = jnp.concatenate([first[near_rows], chosen[near_rows, :512]], axis=1)
         target[:, right] = jnp.concatenate([second[far_rows], chosen[far_rows, 512:]], axis=1)
     sums[...] = jnp.zeros_like(sums)
-    sums[:8, :] = own_gain[...] + arrived[512:520, :128] + arrived[512:520, 128:256]
+    sums[:8, :] = get(6)[...] + arrived[512:520, :128] + arrived[512:520, 128:256]
     high = sums[...].astype(BF)
     low = (sums[...] - high.astype(F32)).astype(BF)
     gain_sum[...] = (high.astype(F32) + low.astype(F32))[:8, :]
@@ -308,6 +308,21 @@
     mean_g = jnp.mean(g, axis=-1, keepdims=True)
     mean_gx = jnp.mean(g * xhat, axis=-1, keepdims=True)
     result[...] = (get(2)[...].astype(F32) + rstd * (g - mean_g - xhat * mean_gx)).astype(BF)
+
+
+def finish_kernel(got, grad_wqkv, grad_wout, grad_gain):
+    total, sums = None, None
+    for s in range(8):
+        part = got[s]
+        for t in range(3):
+            start = t * 1024 + s * 128
+            grad_wqkv[:, start : start + 128] = part[:, t * 128 : (t + 1) * 128]
+        wout = part[:, 384:1408].astype(F32)
+        gain = part[:, 1408:1536].astype(F32) + part[:, 1536:].astype(F32)
+        total = wout if total is None else total + wout
+        sums = gain if sums is None else sums + gain
+    grad_wout[...] = total.astype(BF)
+    grad_gain[...] = sums
 
 
 def high_low(x):
@@ -402,8 +417,7 @@
         + [shape(F32, 128, 1408)] * 2
         + [shape(F32, 8, 128)],
         [pos],
-        [attn, grad_out, attn_twin, grad_twin, wqkv_keep, got],
-        [gain_part],
+        [attn, grad_out, attn_twin, grad_twin, wqkv_keep, got, gain_part],
         scratch=[
             pltpu.VMEM((1024, 1024), F32),
             pltpu.VMEM((512, 1024), F32),
@@ -459,10 +473,15 @@
 
     note = jnp.broadcast_to(packed(gain_sum, 256)[None], (8, 8, 256))
     got = seq_exchange(jnp.concatenate([sums.reshape(8, 8, 1408).astype(BF), note], axis=2))
-    grad_wqkv = got[:, :, :384].reshape(8, 8, 3, head).transpose(1, 2, 0, 3).reshape(8, 3 * width)
-    grad_wout = jnp.sum(got[:, :, 384:1408].astype(F32), axis=0).astype(BF)
-    totals = [unpacked(got[s, :, 1408:]) for s in range(8)]
-    grad_gain = functools.reduce(lambda a, b: a + b, totals).reshape(width)
+    grad_wqkv, grad_wout, grad_gain = call(
+        finish_kernel,
+        "finish",
+        (shape(BF, 8, 3 * width), shape(BF, 8, width), shape(F32, 8, 128)),
+        16 * 1024 * 1024,
+        in_specs=[WHOLE],
+        out_specs=(WHOLE,) * 3,
+    )(got)
+    grad_gain = grad_gain.reshape(width)
     return (
         layer_out[None],
         frame_grad[None],

time: 139 us -> 138 us (level)
  no operation moved by 1% of the time
where the time goes in v1:
time: 138 us; the launch traced here: 137 us
  Pallas kernels  50.9 us (37%)
  starting transfers between devices  41 us (30%)
  waiting for transfers between devices  31.1 us (23%)
  matrix products  9.08 us (7%)
  local copies, waits for them, and re-layouts  1.95 us (1%)
  other arithmetic  1.65 us (1%)
    pallas_call x5, Pallas kernels, staged(): call(kernel, name, tuple(out_shape), vmem, in_specs=[SCALARS] * n + [pl.B...  27.6 us
    pallas_call x1, Pallas kernels, attention(): call(functools.partial(attention_kernel, scale, places), 'attention', (sh...  20.5 us
    all_to_all x4, starting transfers between devices, seq_exchange(): return lax.all_to_all(x, 'seq', 0, 0, tiled=True)  18.9 us
    ppermute x8, waiting for transfers between devices, dp_swap(): return lax.ppermute(x, 'dp', [(i, i ^ bits) for i in range(16)])  17.3 us
    ppermute x9, starting transfers between devices, seq_swap(): return lax.ppermute(x, 'seq', [(i, i ^ bits) for i in range(8)])  12.5 us
    ppermute x8, starting transfers between devices, dp_swap(): return lax.ppermute(x, 'dp', [(i, i ^ bits) for i in range(16)])  9.64 us
    ppermute x9, waiting for transfers between devices, seq_swap(): return lax.ppermute(x, 'seq', [(i, i ^ bits) for i in range(8)])  9.47 us
    dot_general x10, matrix products, mm(): lax.dot_general(a, b, (((ca,), (cb,)), ((), ())), preferred_element_type=...  9.08 us
  transfers between devices with their start and end apart: 21, of which 12 were waited for; matrix products, arithmetic and copies ran while one was open for 7% of the time, Pallas kernels for 17%

profile of v1, /device:TPU:0, one launch (start us, length us, event | category | flops | bytes accessed | tf_op | source)
XLA Modules:
  0.0 136.8 jit_solution(5070607642376548467)
XLA Ops:
  0.6 2.2 %layernorm.1.refs_3_ = bf16[256,1024]{1,0:T(8,128)(2,1)} custom-call(bf16[256,1024]{1,0:T(8,128)(2,1)} %bitcast.37, f32[1,1024]{1,0:T(1,128)} %bitcast.43), custom_call_target="tpu_custom_call" | custom-call | tf_op jit(solution)/shard_map/layernorm/pallas_call | solution.py:358
  2.8 3.1 %collective-permute-start.2 = (bf16[256,1024]{1,0:T(8,128)(2,1)}, bf16[256,1024]{1,0:T(8,128)(2,1)S(1)}, u32[]{:S(2)}, u32[]{:S(2)}) collective-permute-start(bf16[256,1024]{1,0:T(8,128)(2,1)} %layernorm.1.refs_3_), channel_id=1, source_target_pairs={{0,96},{16,112},{32,64},{48,80},{64,32},{80,48},{96,0},{112,16},{1... | collective-permute-start | bytes 1572872 | tf_op jit(solution)/shard_map/ppermute | solution.py:22
  5.9 0.1 collective-permute-start.1
  6.1 1.9 %collective-permute-start = (bf16[256,1024]{1,0:T(8,128)(2,1)}, bf16[256,1024]{1,0:T(8,128)(2,1)}, u32[]{:S(2)}, u32[]{:S(2)}) collective-permute-start(bf16[256,1024]{1,0:T(8,128)(2,1)} %layernorm.1.refs_3_), channel_id=1, source_target_pairs={{0,16},{16,0},{32,48},{48,32},{64,80},{80,64},{96,112},{112,96},{1... | collective-permute-start | bytes 1572872 | tf_op jit(solution)/shard_map/ppermute | solution.py:22
  8.0 0.0 collective-permute-start.9
  8.0 0.6 pad_add_fusion.refs_0_.pos
  8.6 4.6 %dattn.1 = (bf16[8,256,128]{2,1,0:T(8,128)(2,1)}, bf16[1024,384]{1,0:T(8,128)(2,1)}) custom-call(s32[2]{0:T(128)} %pad_add_fusion.refs_0_.pos, bf16[256,1024]{1,0:T(8,128)(2,1)} %bitcast.34, bf16[1024,1024]{1,0:T(8,128)(2,1)} %refs_2_.3, bf16[1024,3072]{1,0:T(8,128)(2,1)} %refs_4_.1), custom_call_target="tpu_custom_call" | custom-call | tf_op jit(solution)/shard_map/dattn/pallas_call | solution.py:84
  13.2 1.6 %convolution_convert_fusion.5.refs_0_ = bf16[256,384]{1,0:T(8,128)(2,1)S(1)} fusion(bf16[256,1024]{1,0:T(8,128)(2,1)S(1)} %copy-done.8, bf16[1024,384]{1,0:T(8,128)(2,1)} %get-tuple-element.30.refs_2_), kind=kOutput, calls=%fused_computation.5 | convolution fusion | flops 201424896 | bytes 1507328 | tf_op jit(solution)/shard_map/dot_general | solution.py:34
  14.8 3.2 %collective-permute-done.2.refs_6_ = bf16[256,1024]{1,0:T(8,128)(2,1)S(1)} collective-permute-done((bf16[256,1024]{1,0:T(8,128)(2,1)}, bf16[256,1024]{1,0:T(8,128)(2,1)S(1)}, u32[]{:S(2)}, u32[]{:S(2)}) %collective-permute-start.2) | collective-permute-done | bytes 524320 | tf_op jit(solution)/shard_map/ppermute | solution.py:22
  18.1 0.4 collective-permute-start.6
  18.5 1.1 collective-permute-done.1.refs_5_
  19.5 1.7 %collective-permute-start.5 = (bf16[128,1024]{1,0:T(8,128)(2,1)S(1)}, bf16[128,1024]{1,0:T(8,128)(2,1)S(1)}, u32[]{:S(2)}, u32[]{:S(2)}) collective-permute-start(bf16[128,1024]{1,0:T(8,128)(2,1)S(1)} %slice.98), channel_id=1, source_target_pairs={{0,96},{16,112},{32,64},{48,80},{64,32},{80,48},{96,0},{112,16},{1... | collective-permute-start | bytes 786440 | tf_op jit(solution)/shard_map/ppermute | solution.py:22
  21.3 0.0 collective-permute-done.refs_4_
  21.3 1.6 %collective-permute-start.4 = (bf16[256,1024]{1,0:T(8,128)(2,1)}, bf16[256,1024]{1,0:T(8,128)(2,1)}, u32[]{:S(2)}, u32[]{:S(2)}) collective-permute-start(bf16[256,1024]{1,0:T(8,128)(2,1)} %collective-permute-done.refs_4_), channel_id=1, source_target_pairs={{0,96},{16,112},{32,64},{48,80},{64,32},{80,48},{96,0},{112,16},{1... | collective-permute-start | bytes 1572872 | tf_op jit(solution)/shard_map/ppermute | solution.py:22
  22.9 0.0 collective-permute-start.3
  22.9 0.4 convolution_convert_fusion.2.refs_3_
  23.3 0.4 convolution_convert_fusion.3.refs_2_
  23.8 1.5 %convolution_convert_fusion.4.refs_1_ = bf16[256,384]{1,0:T(8,128)(2,1)S(1)} fusion(bf16[256,1024]{1,0:T(8,128)(2,1)} %collective-permute-done.refs_4_, bf16[1024,384]{1,0:T(8,128)(2,1)S(1)} %copy-done.7), kind=kOutput, calls=%fused_computation.4 | convolution fusion | flops 201424896 | bytes 1507328 | tf_op jit(solution)/shard_map/dot_general | solution.py:34
  25.2 1.8 %collective-permute-done.6.refs_10_ = bf16[128,1024]{1,0:T(8,128)(2,1)S(1)} collective-permute-done((bf16[128,1024]{1,0:T(8,128)(2,1)S(1)}, bf16[128,1024]{1,0:T(8,128)(2,1)S(1)}, u32[]{:S(2)}, u32[]{:S(2)}) %collective-permute-start.6) | collective-permute-done | bytes 262176 | tf_op jit(solution)/shard_map/ppermute | solution.py:22
  27.1 1.7 %collective-permute-start.8 = (bf16[128,1024]{1,0:T(8,128)(2,1)S(1)}, bf16[128,1024]{1,0:T(8,128)(2,1)S(1)}, u32[]{:S(2)}, u32[]{:S(2)}) collective-permute-start(bf16[128,1024]{1,0:T(8,128)(2,1)S(1)} %collective-permute-done.6.refs_10_), channel_id=1, source_target_pairs={{0,16},{16,0},{32,48},{48,32},{64,80},{80,64},{96,112},{112,96},{1... | collective-permute-start | bytes 786440 | tf_op jit(solution)/shard_map/ppermute | solution.py:22
  28.8 0.3 convolution_convert_fusion.8.refs_7_
  29.1 0.9 collective-permute-done.5.refs_9_
  30.1 1.9 %collective-permute-start.7 = (bf16[128,1024]{1,0:T(8,128)(2,1)S(1)}, bf16[128,1024]{1,0:T(8,128)(2,1)}, u32[]{:S(2)}, u32[]{:S(2)}) collective-permute-start(bf16[128,1024]{1,0:T(8,128)(2,1)S(1)} %collective-permute-done.5.refs_9_), channel_id=1, source_target_pairs={{0,16},{16,0},{32,48},{48,32},{64,80},{80,64},{96,112},{112,96},{1... | collective-permute-start | bytes 786440 | tf_op jit(solution)/shard_map/ppermute | solution.py:22
  32.0 0.3 convolution_convert_fusion.9.refs_6_
  32.3 0.0 collective-permute-done.9.refs_4_
  32.3 2.4 %collective-permute-done.8.refs_12_ = bf16[128,1024]{1,0:T(8,128)(2,1)S(1)} collective-permute-done((bf16[128,1024]{1,0:T(8,128)(2,1)S(1)}, bf16[128,1024]{1,0:T(8,128)(2,1)S(1)}, u32[]{:S(2)}, u32[]{:S(2)}) %collective-permute-start.8) | collective-permute-done | bytes 262176 | tf_op jit(solution)/shard_map/ppermute | solution.py:22
  34.7 5.5 %all-to-all-start = ((bf16[8,256,128]{2,1,0:T(8,128)(2,1)}), bf16[8,256,128]{2,1,0:T(8,128)(2,1)S(1)}, u32[]{:S(2)}, u32[]{:S(2)}) async-start(bf16[8,256,128]{2,1,0:T(8,128)(2,1)} %get-tuple-element.32), calls=%async_computation | async-start | bytes 1048576 | tf_op jit(solution)/shard_map/all_to_all | solution.py:30
  40.2 0.3 convolution_convert_fusion.6.refs_9_
  40.5 0.0 copy-start.3
  40.5 0.0 copy-start.4
  40.5 0.0 collective-permute-done.4.refs_8_
  40.6 1.5 %convolution_convert_fusion.refs_5_ = bf16[256,384]{1,0:T(8,128)(2,1)S(1)} fusion(bf16[256,1024]{1,0:T(8,128)(2,1)} %collective-permute-done.4.refs_8_, bf16[1024,384]{1,0:T(8,128)(2,1)S(1)} %copy-done.7), kind=kOutput, calls=%fused_computation | convolution fusion | flops 201424896 | bytes 1507328 | tf_op jit(solution)/shard_map/dot_general | solution.py:34
  42.0 1.2 convolution_convert_fusion.7.refs_8_
  43.3 0.0 collective-permute-done.3.refs_7_
  43.3 1.5 %convolution_convert_fusion.1.refs_4_ = bf16[256,384]{1,0:T(8,128)(2,1)S(1)} fusion(bf16[256,1024]{1,0:T(8,128)(2,1)} %collective-permute-done.3.refs_7_, bf16[1024,384]{1,0:T(8,128)(2,1)S(1)} %copy-done.7), kind=kOutput, calls=%fused_computation.1 | convolution fusion | flops 201424896 | bytes 1507328 | tf_op jit(solution)/shard_map/dot_general | solution.py:34
  44.8 3.6 %all-to-all-done.refs_10_ = bf16[8,256,128]{2,1,0:T(8,128)(2,1)S(1)} async-done(((bf16[8,256,128]{2,1,0:T(8,128)(2,1)}), bf16[8,256,128]{2,1,0:T(8,128)(2,1)S(1)}, u32[]{:S(2)}, u32[]{:S(2)}) %all-to-all-start) | async-done | bytes 524320 | tf_op jit(solution)/shard_map/all_to_all | solution.py:30
  48.4 20.5 %attention.1 = (bf16[2048,128]{1,0:T(8,128)(2,1)}, bf16[2048,384]{1,0:T(8,128)(2,1)}) custom-call(s32[2]{0:T(128)S(1)} %copy-done.4, bf16[256,384]{1,0:T(8,128)(2,1)S(1)} %convolution_convert_fusion.5.refs_0_, bf16[256,384]{1,0:T(8,128)(2,1)S(1)} %convolution_convert_fusion.4.refs_1_, bf16[256,384]{1,0:T(8,128)(2,1)S(1)} %convolution_convert_fusion.3.refs_2_, ...), custom_call_target="tpu_custom_call" | custom-call | tf_op jit(solution)/shard_map/attention/pallas_call | solution.py:194
  68.9 3.7 %all-to-all-start.1 = ((bf16[8,256,128]{2,1,0:T(8,128)(2,1)}), bf16[8,256,128]{2,1,0:T(8,128)(2,1)S(1)}, u32[]{:S(2)}, u32[]{:S(2)}) async-start(bf16[8,256,128]{2,1,0:T(8,128)(2,1)} %bitcast.5), calls=%async_computation.1 | async-start | bytes 1048576 | tf_op jit(solution)/shard_map/all_to_all | solution.py:30
  72.6 0.0 copy-start
  72.6 0.0 copy-start.5
  72.6 7.1 %projection_gradient.1 = (f32[512,384]{1,0:T(8,128)}, bf16[528,384]{1,0:T(8,128)(2,1)}, f32[8,128]{1,0:T(8,128)}) custom-call(s32[2]{0:T(128)} %pad_add_fusion.refs_0_.pos, bf16[2048,384]{1,0:T(8,128)(2,1)} %get-tuple-element.34.refs_1_, bf16[1024,384]{1,0:T(8,128)(2,1)} %get-tuple-element.30.refs_2_, bf16[256,1024]{1,0:T(8,128)(2,1)} %layernorm.1.refs_3_, ...), custom_call_target="tpu_custom_call" | custom-call | tf_op jit(solution)/shard_map/projection_gradient/pallas_call | solution.py:84
  79.7 0.7 all-to-all-done.1.refs_1_
  80.5 0.5 collective-permute-start.11
  81.0 2.1 %collective-permute-done.11.refs_6_ = bf16[528,384]{1,0:T(8,128)(2,1)S(1)} collective-permute-done((bf16[528,384]{1,0:T(8,128)(2,1)}, bf16[528,384]{1,0:T(8,128)(2,1)S(1)}, u32[]{:S(2)}, u32[]{:S(2)}) %collective-permute-start.11) | collective-permute-done | bytes 405536 | tf_op jit(solution)/shard_map/ppermute | solution.py:26
  83.0 0.0 collective-permute-done.10.refs_3_
  83.0 1.1 copy-done.2
  84.2 0.7 copy-done.6
  84.8 3.8 %output_gradient.1 = (bf16[272,640]{1,0:T(8,128)(2,1)}, bf16[256,768]{1,0:T(8,128)(2,1)S(1)}, f32[128,1408]{1,0:T(8,128)S(1)}, f32[128,1408]{1,0:T(8,128)S(1)}, f32[8,128]{1,0:T(8,128)S(1)}) custom-call(s32[2]{0:T(128)S(1)} %copy-done.5, bf16[8,256,128]{2,1,0:T(8,128)(2,1)S(1)} %all-to-all-done.1.refs_1_, bf16[256,1024]{1,0:T(8,128)(2,1)S(1)} %bitcast.36, ...), custom_call_target="tpu_custom_call" | custom-call | tf_op jit(solution)/shard_map/output_gradient/pallas_call | solution.py:84
  88.7 2.8 %collective-permute-start.13 = (bf16[256,768]{1,0:T(8,128)(2,1)S(1)}, bf16[256,768]{1,0:T(8,128)(2,1)S(1)}, u32[]{:S(2)}, u32[]{:S(2)}) collective-permute-start(bf16[256,768]{1,0:T(8,128)(2,1)S(1)} %get-tuple-element.43), channel_id=1, source_target_pairs={{0,12},{1,13},{2,14},{3,15},{4,8},{5,9},{6,10},{7,11},{8,4},{9,5},... | collective-permute-start | bytes 1179656 | tf_op jit(solution)/shard_map/ppermute | solution.py:26
  91.5 0.2 collective-permute-start.12
  91.7 4.9 %all-to-all-start.2 = ((bf16[8,256,384]{2,1,0:T(8,128)(2,1)}), bf16[8,256,384]{2,1,0:T(8,128)(2,1)}, u32[]{:S(2)}, u32[]{:S(2)}) async-start(bf16[8,256,384]{2,1,0:T(8,128)(2,1)} %bitcast.7), calls=%async_computation.2 | async-start | bytes 3145728 | tf_op jit(solution)/shard_map/all_to_all | solution.py:30
  96.6 3.5 %layer_out.1 = bf16[256,1024]{1,0:T(8,128)(2,1)} custom-call(bf16[256,1024]{1,0:T(8,128)(2,1)} %bitcast.38, bf16[8,256,128]{2,1,0:T(8,128)(2,1)} %copy-done.1, bf16[1024,1024]{1,0:T(8,128)(2,1)} %refs_2_.3), custom_call_target="tpu_custom_call" | custom-call | tf_op jit(solution)/shard_map/layer_out/pallas_call | solution.py:84
  100.1 1.5 %collective-permute-done.12 = bf16[272,640]{1,0:T(8,128)(2,1)S(1)} collective-permute-done((bf16[272,640]{1,0:T(8,128)(2,1)}, bf16[272,640]{1,0:T(8,128)(2,1)S(1)}, u32[]{:S(2)}, u32[]{:S(2)}) %collective-permute-start.12) | collective-permute-done | bytes 348192 | tf_op jit(solution)/shard_map/ppermute | solution.py:26
  101.7 2.3 %collective-permute-start.14 = (bf16[136,640]{1,0:T(8,128)(2,1)S(1)}, bf16[136,640]{1,0:T(8,128)(2,1)S(1)}, u32[]{:S(2)}, u32[]{:S(2)}) collective-permute-start(bf16[136,640]{1,0:T(8,128)(2,1)S(1)} %pad_maximum_fusion.3), channel_id=1, source_target_pairs={{0,12},{1,13},{2,14},{3,15},{4,8},{5,9},{6,10},{7,11},{8,4},{9,5},... | collective-permute-start | bytes 522248 | tf_op jit(solution)/shard_map/ppermute | solution.py:26
  104.1 0.1 collective-permute-start.15
  104.2 4.3 %collective-permute-done.14 = bf16[136,640]{1,0:T(8,128)(2,1)S(1)} collective-permute-done((bf16[136,640]{1,0:T(8,128)(2,1)S(1)}, bf16[136,640]{1,0:T(8,128)(2,1)S(1)}, u32[]{:S(2)}, u32[]{:S(2)}) %collective-permute-start.14) | collective-permute-done | bytes 174112 | tf_op jit(solution)/shard_map/ppermute | solution.py:26
  108.5 1.5 %collective-permute-done.15 = bf16[128,768]{1,0:T(8,128)(2,1)S(1)} collective-permute-done((bf16[128,768]{1,0:T(8,128)(2,1)S(1)}, bf16[128,768]{1,0:T(8,128)(2,1)S(1)}, u32[]{:S(2)}, u32[]{:S(2)}) %collective-permute-start.15) | collective-permute-done | bytes 196640 | tf_op jit(solution)/shard_map/ppermute | solution.py:26
  110.0 0.1 maximum_add_fusion
  110.2 3.7 %collective-permute-start.16 = (bf16[72,1408]{1,0:T(8,128)(2,1)S(1)}, bf16[72,1408]{1,0:T(8,128)(2,1)S(1)}, u32[]{:S(2)}, u32[]{:S(2)}) collective-permute-start(bf16[72,1408]{1,0:T(8,128)(2,1)S(1)} %pad_maximum_fusion.2), channel_id=1, source_target_pairs={{0,2},{1,3},{2,0},{3,1},{4,6},{5,7},{6,4},{7,5},{8,10},{9,11},{10,... | collective-permute-start | bytes 608264 | tf_op jit(solution)/shard_map/ppermute | solution.py:26
  113.8 8.0 %collective-permute-done.16 = bf16[72,1408]{1,0:T(8,128)(2,1)S(1)} collective-permute-done((bf16[72,1408]{1,0:T(8,128)(2,1)S(1)}, bf16[72,1408]{1,0:T(8,128)(2,1)S(1)}, u32[]{:S(2)}, u32[]{:S(2)}) %collective-permute-start.16) | collective-permute-done | bytes 202784 | tf_op jit(solution)/shard_map/ppermute | solution.py:26
  122.0 0.7 pad_maximum_fusion.1
  122.7 4.8 %all-to-all-start.3 = ((bf16[8,8,1664]{2,1,0:T(8,128)(2,1)}), bf16[8,8,1664]{2,1,0:T(8,128)(2,1)S(1)}, u32[]{:S(2)}, u32[]{:S(2)}) async-start(bf16[8,8,1664]{2,1,0:T(8,128)(2,1)} %pad_maximum_fusion.1), calls=%async_computation.3 | async-start | bytes 425984 | tf_op jit(solution)/shard_map/all_to_all | solution.py:30
  127.5 8.7 %frame_gradient.1 = bf16[256,1024]{1,0:T(8,128)(2,1)} custom-call(bf16[256,1024]{1,0:T(8,128)(2,1)} %bitcast.39, bf16[8,256,384]{2,1,0:T(8,128)(2,1)} %all-to-all-done.2.refs_1_, bf16[256,1024]{1,0:T(8,128)(2,1)} %bitcast.35, f32[1,1024]{1,0:T(1,128)} %bitcast.45, bf16[1024,3072]{1,0:T(8,128)(2,1)} %refs_4_.1), custom_call_target="tpu_custom_call" | custom-call | tf_op jit(solution)/shard_map/frame_gradient/pallas_call | solution.py:84
  136.2 0.7 finish.1
  (49 shorter events, 0.4 us)
Async XLA Ops:
  2.8 15.2 %collective-permute-start.2 = (bf16[256,1024]{1,0:T(8,128)(2,1)}, bf16[256,1024]{1,0:T(8,128)(2,1)S(1)}, u32[]{:S(2)}, u32[]{:S(2)}) collective-permute-start(bf16[256,1024]{1,0:T(8,128)(2,1)} %layernorm.1.refs_3_), channel_id=1, source_target_pairs={{0,96},{16,112},{32,64},{48,80},{64,32},{80,48},{96,0},{112,16},{1... | collective-permute-start | bytes 1572872 | tf_op jit(solution)/shard_map/ppermute | solution.py:22
  5.9 13.6 %collective-permute-start.1 = (bf16[256,1024]{1,0:T(8,128)(2,1)}, bf16[256,1024]{1,0:T(8,128)(2,1)S(1)}, u32[]{:S(2)}, u32[]{:S(2)}) collective-permute-start(bf16[256,1024]{1,0:T(8,128)(2,1)} %layernorm.1.refs_3_), channel_id=1, source_target_pairs={{0,32},{16,48},{32,0},{48,16},{64,96},{80,112},{96,64},{112,80},{1... | collective-permute-start | bytes 1572872 | tf_op jit(solution)/shard_map/ppermute | solution.py:22
  6.1 15.2 %collective-permute-start = (bf16[256,1024]{1,0:T(8,128)(2,1)}, bf16[256,1024]{1,0:T(8,128)(2,1)}, u32[]{:S(2)}, u32[]{:S(2)}) collective-permute-start(bf16[256,1024]{1,0:T(8,128)(2,1)} %layernorm.1.refs_3_), channel_id=1, source_target_pairs={{0,16},{16,0},{32,48},{48,32},{64,80},{80,64},{96,112},{112,96},{1... | collective-permute-start | bytes 1572872 | tf_op jit(solution)/shard_map/ppermute | solution.py:22
  8.0 24.3 %collective-permute-start.9 = (bf16[256,1024]{1,0:T(8,128)(2,1)}, bf16[256,1024]{1,0:T(8,128)(2,1)S(1)}, u32[]{:S(2)}, u32[]{:S(2)}) collective-permute-start(bf16[256,1024]{1,0:T(8,128)(2,1)} %bitcast.33), channel_id=1, source_target_pairs={{0,1},{1,0},{2,3},{3,2},{4,5},{5,4},{6,7},{7,6},{8,9},{9,8},{10,11... | collective-permute-start | bytes 1572872 | tf_op jit(solution)/shard_map/ppermute | solution.py:26
  8.6 4.6 %copy-start.8 = (bf16[256,1024]{1,0:T(8,128)(2,1)S(1)}, bf16[256,1024]{1,0:T(8,128)(2,1)}, u32[]{:S(2)}) copy-start(bf16[256,1024]{1,0:T(8,128)(2,1)} %layernorm.1.refs_3_) | copy-start | bytes 1572868
  13.2 9.7 %copy-start.7 = (bf16[1024,384]{1,0:T(8,128)(2,1)S(1)}, bf16[1024,384]{1,0:T(8,128)(2,1)}, u32[]{:S(2)}) copy-start(bf16[1024,384]{1,0:T(8,128)(2,1)} %get-tuple-element.30.refs_2_) | copy-start | bytes 2359300
  18.1 4.8 %copy-start.9 = (bf16[256,1024]{1,0:T(8,128)(2,1)}, bf16[256,1024]{1,0:T(8,128)(2,1)S(1)}, u32[]{:S(2)}) copy-start(bf16[256,1024]{1,0:T(8,128)(2,1)S(1)} %collective-permute-done.2.refs_6_) | copy-start | bytes 1572868
  18.1 9.0 %collective-permute-start.6 = (bf16[128,1024]{1,0:T(8,128)(2,1)S(1)}, bf16[128,1024]{1,0:T(8,128)(2,1)S(1)}, u32[]{:S(2)}, u32[]{:S(2)}) collective-permute-start(bf16[128,1024]{1,0:T(8,128)(2,1)S(1)} %slice.99), channel_id=1, source_target_pairs={{0,32},{16,48},{32,0},{48,16},{64,96},{80,112},{96,64},{112,80},{1... | collective-permute-start | bytes 786440 | tf_op jit(solution)/shard_map/ppermute | solution.py:22
  19.5 5.7 %copy-start.10 = (bf16[256,1024]{1,0:T(8,128)(2,1)}, bf16[256,1024]{1,0:T(8,128)(2,1)S(1)}, u32[]{:S(2)}) copy-start(bf16[256,1024]{1,0:T(8,128)(2,1)S(1)} %collective-permute-done.1.refs_5_) | copy-start | bytes 1572868
  19.5 10.5 %collective-permute-start.5 = (bf16[128,1024]{1,0:T(8,128)(2,1)S(1)}, bf16[128,1024]{1,0:T(8,128)(2,1)S(1)}, u32[]{:S(2)}, u32[]{:S(2)}) collective-permute-start(bf16[128,1024]{1,0:T(8,128)(2,1)S(1)} %slice.98), channel_id=1, source_target_pairs={{0,96},{16,112},{32,64},{48,80},{64,32},{80,48},{96,0},{112,16},{1... | collective-permute-start | bytes 786440 | tf_op jit(solution)/shard_map/ppermute | solution.py:22
  21.3 19.3 %collective-permute-start.4 = (bf16[256,1024]{1,0:T(8,128)(2,1)}, bf16[256,1024]{1,0:T(8,128)(2,1)}, u32[]{:S(2)}, u32[]{:S(2)}) collective-permute-start(bf16[256,1024]{1,0:T(8,128)(2,1)} %collective-permute-done.refs_4_), channel_id=1, source_target_pairs={{0,96},{16,112},{32,64},{48,80},{64,32},{80,48},{96,0},{112,16},{1... | collective-permute-start | bytes 1572872 | tf_op jit(solution)/shard_map/ppermute | solution.py:22
  22.9 20.4 %collective-permute-start.3 = (bf16[256,1024]{1,0:T(8,128)(2,1)}, bf16[256,1024]{1,0:T(8,128)(2,1)}, u32[]{:S(2)}, u32[]{:S(2)}) collective-permute-start(bf16[256,1024]{1,0:T(8,128)(2,1)} %collective-permute-done.refs_4_), channel_id=1, source_target_pairs={{0,32},{16,48},{32,0},{48,16},{64,96},{80,112},{96,64},{112,80},{1... | collective-permute-start | bytes 1572872 | tf_op jit(solution)/shard_map/ppermute | solution.py:22
  27.1 5.2 %copy-start.11 = (bf16[128,1024]{1,0:T(8,128)(2,1)}, bf16[128,1024]{1,0:T(8,128)(2,1)S(1)}, u32[]{:S(2)}) copy-start(bf16[128,1024]{1,0:T(8,128)(2,1)S(1)} %collective-permute-done.6.refs_10_) | copy-start | bytes 786436
  27.1 7.7 %collective-permute-start.8 = (bf16[128,1024]{1,0:T(8,128)(2,1)S(1)}, bf16[128,1024]{1,0:T(8,128)(2,1)S(1)}, u32[]{:S(2)}, u32[]{:S(2)}) collective-permute-start(bf16[128,1024]{1,0:T(8,128)(2,1)S(1)} %collective-permute-done.6.refs_10_), channel_id=1, source_target_pairs={{0,16},{16,0},{32,48},{48,32},{64,80},{80,64},{96,112},{112,96},{1... | collective-permute-start | bytes 786440 | tf_op jit(solution)/shard_map/ppermute | solution.py:22
  30.1 12.0 %copy-start.12 = (bf16[128,1024]{1,0:T(8,128)(2,1)}, bf16[128,1024]{1,0:T(8,128)(2,1)S(1)}, u32[]{:S(2)}) copy-start(bf16[128,1024]{1,0:T(8,128)(2,1)S(1)} %collective-permute-done.5.refs_9_) | copy-start | bytes 786436
  30.1 12.0 %collective-permute-start.7 = (bf16[128,1024]{1,0:T(8,128)(2,1)S(1)}, bf16[128,1024]{1,0:T(8,128)(2,1)}, u32[]{:S(2)}, u32[]{:S(2)}) collective-permute-start(bf16[128,1024]{1,0:T(8,128)(2,1)S(1)} %collective-permute-done.5.refs_9_), channel_id=1, source_target_pairs={{0,16},{16,0},{32,48},{48,32},{64,80},{80,64},{96,112},{112,96},{1... | collective-permute-start | bytes 786440 | tf_op jit(solution)/shard_map/ppermute | solution.py:22
  34.7 5.8 %copy-start.13 = (bf16[128,1024]{1,0:T(8,128)(2,1)}, bf16[128,1024]{1,0:T(8,128)(2,1)S(1)}, u32[]{:S(2)}) copy-start(bf16[128,1024]{1,0:T(8,128)(2,1)S(1)} %collective-permute-done.8.refs_12_) | copy-start | bytes 786436
  34.7 13.7 %all-to-all-start = ((bf16[8,256,128]{2,1,0:T(8,128)(2,1)}), bf16[8,256,128]{2,1,0:T(8,128)(2,1)S(1)}, u32[]{:S(2)}, u32[]{:S(2)}) async-start(bf16[8,256,128]{2,1,0:T(8,128)(2,1)} %get-tuple-element.32), calls=%async_computation | async-start | bytes 1048576 | tf_op jit(solution)/shard_map/all_to_all | solution.py:30
  40.5 7.9 %copy-start.3 = (s32[1,2048]{1,0:T(1,128)S(1)}, s32[1,2048]{1,0:T(1,128)}, u32[]{:S(2)}) copy-start(s32[1,2048]{1,0:T(1,128)} %refs_11_.1) | copy-start | bytes 24580
  40.5 7.9 %copy-start.4 = (s32[2]{0:T(128)S(1)}, s32[2]{0:T(128)}, u32[]{:S(2)}) copy-start(s32[2]{0:T(128)} %pad_add_fusion.refs_0_.pos) | copy-start | bytes 28
  68.9 11.6 %all-to-all-start.1 = ((bf16[8,256,128]{2,1,0:T(8,128)(2,1)}), bf16[8,256,128]{2,1,0:T(8,128)(2,1)S(1)}, u32[]{:S(2)}, u32[]{:S(2)}) async-start(bf16[8,256,128]{2,1,0:T(8,128)(2,1)} %bitcast.5), calls=%async_computation.1 | async-start | bytes 1048576 | tf_op jit(solution)/shard_map/all_to_all | solution.py:30
  72.6 10.4 %copy-start = (bf16[1,256,1024]{2,1,0:T(8,128)(2,1)S(1)}, bf16[1,256,1024]{2,1,0:T(8,128)(2,1)}, u32[]{:S(2)}) copy-start(bf16[1,256,1024]{2,1,0:T(8,128)(2,1)} %param.11) | copy-start | bytes 1572868
  72.6 10.4 %copy-start.5 = (s32[2]{0:T(128)S(1)}, s32[2]{0:T(128)}, u32[]{:S(2)}) copy-start(s32[2]{0:T(128)} %pad_add_fusion.refs_0_.pos) | copy-start | bytes 28
  80.4 11.3 %copy-start.1 = (bf16[8,256,128]{2,1,0:T(8,128)(2,1)}, bf16[8,256,128]{2,1,0:T(8,128)(2,1)S(1)}, u32[]{:S(2)}) copy-start(bf16[8,256,128]{2,1,0:T(8,128)(2,1)S(1)} %all-to-all-done.1.refs_1_) | copy-start | bytes 1572868
  80.4 2.6 %collective-permute-start.10 = (bf16[8,256,128]{2,1,0:T(8,128)(2,1)S(1)}, bf16[8,256,128]{2,1,0:T(8,128)(2,1)S(1)}, u32[]{:S(2)}, u32[]{:S(2)}) collective-permute-start(bf16[8,256,128]{2,1,0:T(8,128)(2,1)S(1)} %all-to-all-done.1.refs_1_), channel_id=1, source_target_pairs={{0,1},{1,0},{2,3},{3,2},{4,5},{5,4},{6,7},{7,6},{8,9},{9,8},{10,11... | collective-permute-start | bytes 1572872 | tf_op jit(solution)/shard_map/ppermute | solution.py:26
  80.5 2.6 %collective-permute-start.11 = (bf16[528,384]{1,0:T(8,128)(2,1)}, bf16[528,384]{1,0:T(8,128)(2,1)S(1)}, u32[]{:S(2)}, u32[]{:S(2)}) collective-permute-start(bf16[528,384]{1,0:T(8,128)(2,1)} %get-tuple-element.40), channel_id=1, source_target_pairs={{0,1},{1,0},{2,3},{3,2},{4,5},{5,4},{6,7},{7,6},{8,9},{9,8},{10,11... | collective-permute-start | bytes 1216520 | tf_op jit(solution)/shard_map/ppermute | solution.py:26
  83.0 1.1 copy-start.2
  84.2 0.7 copy-start.6
  88.7 13.0 %collective-permute-start.13 = (bf16[256,768]{1,0:T(8,128)(2,1)S(1)}, bf16[256,768]{1,0:T(8,128)(2,1)S(1)}, u32[]{:S(2)}, u32[]{:S(2)}) collective-permute-start(bf16[256,768]{1,0:T(8,128)(2,1)S(1)} %get-tuple-element.43), channel_id=1, source_target_pairs={{0,12},{1,13},{2,14},{3,15},{4,8},{5,9},{6,10},{7,11},{8,4},{9,5},... | collective-permute-start | bytes 1179656 | tf_op jit(solution)/shard_map/ppermute | solution.py:26
  91.5 10.1 %collective-permute-start.12 = (bf16[272,640]{1,0:T(8,128)(2,1)}, bf16[272,640]{1,0:T(8,128)(2,1)S(1)}, u32[]{:S(2)}, u32[]{:S(2)}) collective-permute-start(bf16[272,640]{1,0:T(8,128)(2,1)} %get-tuple-element.42), channel_id=1, source_target_pairs={{0,4},{1,5},{2,6},{3,7},{4,0},{5,1},{6,2},{7,3},{8,12},{9,13},{10,... | collective-permute-start | bytes 1044488 | tf_op jit(solution)/shard_map/ppermute | solution.py:26
  91.7 30.2 %all-to-all-start.2 = ((bf16[8,256,384]{2,1,0:T(8,128)(2,1)}), bf16[8,256,384]{2,1,0:T(8,128)(2,1)}, u32[]{:S(2)}, u32[]{:S(2)}) async-start(bf16[8,256,384]{2,1,0:T(8,128)(2,1)} %bitcast.7), calls=%async_computation.2 | async-start | bytes 3145728 | tf_op jit(solution)/shard_map/all_to_all | solution.py:30
  101.7 6.7 %collective-permute-start.14 = (bf16[136,640]{1,0:T(8,128)(2,1)S(1)}, bf16[136,640]{1,0:T(8,128)(2,1)S(1)}, u32[]{:S(2)}, u32[]{:S(2)}) collective-permute-start(bf16[136,640]{1,0:T(8,128)(2,1)S(1)} %pad_maximum_fusion.3), channel_id=1, source_target_pairs={{0,12},{1,13},{2,14},{3,15},{4,8},{5,9},{6,10},{7,11},{8,4},{9,5},... | collective-permute-start | bytes 522248 | tf_op jit(solution)/shard_map/ppermute | solution.py:26
  104.1 5.9 %collective-permute-start.15 = (bf16[128,768]{1,0:T(8,128)(2,1)S(1)}, bf16[128,768]{1,0:T(8,128)(2,1)S(1)}, u32[]{:S(2)}, u32[]{:S(2)}) collective-permute-start(bf16[128,768]{1,0:T(8,128)(2,1)S(1)} %add_convert_fusion), channel_id=1, source_target_pairs={{0,4},{1,5},{2,6},{3,7},{4,0},{5,1},{6,2},{7,3},{8,12},{9,13},{10,... | collective-permute-start | bytes 589832 | tf_op jit(solution)/shard_map/ppermute | solution.py:26
  110.2 11.7 %collective-permute-start.16 = (bf16[72,1408]{1,0:T(8,128)(2,1)S(1)}, bf16[72,1408]{1,0:T(8,128)(2,1)S(1)}, u32[]{:S(2)}, u32[]{:S(2)}) collective-permute-start(bf16[72,1408]{1,0:T(8,128)(2,1)S(1)} %pad_maximum_fusion.2), channel_id=1, source_target_pairs={{0,2},{1,3},{2,0},{3,1},{4,6},{5,7},{6,4},{7,5},{8,10},{9,11},{10,... | collective-permute-start | bytes 608264 | tf_op jit(solution)/shard_map/ppermute | solution.py:26
  122.7 13.5 %all-to-all-start.3 = ((bf16[8,8,1664]{2,1,0:T(8,128)(2,1)}), bf16[8,8,1664]{2,1,0:T(8,128)(2,1)S(1)}, u32[]{:S(2)}, u32[]{:S(2)}) async-start(bf16[8,8,1664]{2,1,0:T(8,128)(2,1)} %pad_maximum_fusion.1), calls=%async_computation.3 | async-start | bytes 425984 | tf_op jit(solution)/shard_map/all_to_all | solution.py:30

commit v2 on v1

--- a/solution.py
+++ b/solution.py
@@ -11,7 +11,7 @@
 BF = jnp.bfloat16
 F32 = jnp.float32
 LOG2E = 1.4426950408889634
-PAIR = 4
+PAIR = 8
 CHUNK = 256
 VMEM_LIMIT = 60 * 1024 * 1024
 WHOLE = pl.BlockSpec(memory_space=pltpu.VMEM)

time: 138 us -> 138 us (level)
  no operation moved by 1% of the time
where the time goes in v2:
time: 138 us; the launch traced here: 136 us
  Pallas kernels  50.4 us (37%)
  starting transfers between devices  40.8 us (30%)
  waiting for transfers between devices  31.3 us (23%)
  matrix products  9.08 us (7%)
  local copies, waits for them, and re-layouts  1.95 us (1%)
  other arithmetic  1.65 us (1%)
    pallas_call x5, Pallas kernels, staged(): call(kernel, name, tuple(out_shape), vmem, in_specs=[SCALARS] * n + [pl.B...  27.6 us
    pallas_call x1, Pallas kernels, attention(): call(functools.partial(attention_kernel, scale, places), 'attention', (sh...  19.9 us
    all_to_all x4, starting transfers between devices, seq_exchange(): return lax.all_to_all(x, 'seq', 0, 0, tiled=True)  18.7 us
    ppermute x8, waiting for transfers between devices, dp_swap(): return lax.ppermute(x, 'dp', [(i, i ^ bits) for i in range(16)])  17.3 us
    ppermute x9, starting transfers between devices, seq_swap(): return lax.ppermute(x, 'seq', [(i, i ^ bits) for i in range(8)])  12.5 us
    ppermute x8, starting transfers between devices, dp_swap(): return lax.ppermute(x, 'dp', [(i, i ^ bits) for i in range(16)])  9.64 us
    ppermute x9, waiting for transfers between devices, seq_swap(): return lax.ppermute(x, 'seq', [(i, i ^ bits) for i in range(8)])  9.47 us
    dot_general x10, matrix products, mm(): lax.dot_general(a, b, (((ca,), (cb,)), ((), ())), preferred_element_type=...  9.08 us
  transfers between devices with their start and end apart: 21, of which 12 were waited for; matrix products, arithmetic and copies ran while one was open for 7% of the time, Pallas kernels for 17%

profile of v2, /device:TPU:0, one launch (start us, length us, event | category | flops | bytes accessed | tf_op | source)
XLA Modules:
  0.0 136.3 jit_solution(239363527922883962)
XLA Ops:
  0.6 2.2 %layernorm.1.refs_3_ = bf16[256,1024]{1,0:T(8,128)(2,1)} custom-call(bf16[256,1024]{1,0:T(8,128)(2,1)} %bitcast.37, f32[1,1024]{1,0:T(1,128)} %bitcast.43), custom_call_target="tpu_custom_call" | custom-call | tf_op jit(solution)/shard_map/layernorm/pallas_call | solution.py:358
  2.8 3.1 %collective-permute-start.2 = (bf16[256,1024]{1,0:T(8,128)(2,1)}, bf16[256,1024]{1,0:T(8,128)(2,1)S(1)}, u32[]{:S(2)}, u32[]{:S(2)}) collective-permute-start(bf16[256,1024]{1,0:T(8,128)(2,1)} %layernorm.1.refs_3_), channel_id=1, source_target_pairs={{0,96},{16,112},{32,64},{48,80},{64,32},{80,48},{96,0},{112,16},{1... | collective-permute-start | bytes 1572872 | tf_op jit(solution)/shard_map/ppermute | solution.py:22
  5.9 0.1 collective-permute-start.1
  6.1 1.9 %collective-permute-start = (bf16[256,1024]{1,0:T(8,128)(2,1)}, bf16[256,1024]{1,0:T(8,128)(2,1)}, u32[]{:S(2)}, u32[]{:S(2)}) collective-permute-start(bf16[256,1024]{1,0:T(8,128)(2,1)} %layernorm.1.refs_3_), channel_id=1, source_target_pairs={{0,16},{16,0},{32,48},{48,32},{64,80},{80,64},{96,112},{112,96},{1... | collective-permute-start | bytes 1572872 | tf_op jit(solution)/shard_map/ppermute | solution.py:22
  8.0 0.6 pad_add_fusion.refs_0_.pos
  8.6 4.6 %dattn.1 = (bf16[8,256,128]{2,1,0:T(8,128)(2,1)}, bf16[1024,384]{1,0:T(8,128)(2,1)}) custom-call(s32[2]{0:T(128)} %pad_add_fusion.refs_0_.pos, bf16[256,1024]{1,0:T(8,128)(2,1)} %bitcast.34, bf16[1024,1024]{1,0:T(8,128)(2,1)} %refs_2_.3, bf16[1024,3072]{1,0:T(8,128)(2,1)} %refs_4_.1), custom_call_target="tpu_custom_call" | custom-call | tf_op jit(solution)/shard_map/dattn/pallas_call | solution.py:84
  13.2 1.6 %convolution_convert_fusion.5.refs_0_ = bf16[256,384]{1,0:T(8,128)(2,1)S(1)} fusion(bf16[256,1024]{1,0:T(8,128)(2,1)S(1)} %copy-done.8, bf16[1024,384]{1,0:T(8,128)(2,1)} %get-tuple-element.30.refs_2_), kind=kOutput, calls=%fused_computation.5 | convolution fusion | flops 201424896 | bytes 1507328 | tf_op jit(solution)/shard_map/dot_general | solution.py:34
  14.8 3.2 %collective-permute-done.2.refs_6_ = bf16[256,1024]{1,0:T(8,128)(2,1)S(1)} collective-permute-done((bf16[256,1024]{1,0:T(8,128)(2,1)}, bf16[256,1024]{1,0:T(8,128)(2,1)S(1)}, u32[]{:S(2)}, u32[]{:S(2)}) %collective-permute-start.2) | collective-permute-done | bytes 524320 | tf_op jit(solution)/shard_map/ppermute | solution.py:22
  18.1 0.4 collective-permute-start.6
  18.5 1.1 collective-permute-done.1.refs_5_
  19.5 1.7 %collective-permute-start.5 = (bf16[128,1024]{1,0:T(8,128)(2,1)S(1)}, bf16[128,1024]{1,0:T(8,128)(2,1)S(1)}, u32[]{:S(2)}, u32[]{:S(2)}) collective-permute-start(bf16[128,1024]{1,0:T(8,128)(2,1)S(1)} %slice.98), channel_id=1, source_target_pairs={{0,96},{16,112},{32,64},{48,80},{64,32},{80,48},{96,0},{112,16},{1... | collective-permute-start | bytes 786440 | tf_op jit(solution)/shard_map/ppermute | solution.py:22
  21.3 0.0 collective-permute-done.refs_4_
  21.3 1.6 %collective-permute-start.4 = (bf16[256,1024]{1,0:T(8,128)(2,1)}, bf16[256,1024]{1,0:T(8,128)(2,1)}, u32[]{:S(2)}, u32[]{:S(2)}) collective-permute-start(bf16[256,1024]{1,0:T(8,128)(2,1)} %collective-permute-done.refs_4_), channel_id=1, source_target_pairs={{0,96},{16,112},{32,64},{48,80},{64,32},{80,48},{96,0},{112,16},{1... | collective-permute-start | bytes 1572872 | tf_op jit(solution)/shard_map/ppermute | solution.py:22
  22.9 0.0 collective-permute-start.3
  22.9 0.4 convolution_convert_fusion.2.refs_3_
  23.3 0.4 convolution_convert_fusion.3.refs_2_
  23.8 1.5 %convolution_convert_fusion.4.refs_1_ = bf16[256,384]{1,0:T(8,128)(2,1)S(1)} fusion(bf16[256,1024]{1,0:T(8,128)(2,1)} %collective-permute-done.refs_4_, bf16[1024,384]{1,0:T(8,128)(2,1)S(1)} %copy-done.7), kind=kOutput, calls=%fused_computation.4 | convolution fusion | flops 201424896 | bytes 1507328 | tf_op jit(solution)/shard_map/dot_general | solution.py:34
  25.2 1.8 %collective-permute-done.6.refs_10_ = bf16[128,1024]{1,0:T(8,128)(2,1)S(1)} collective-permute-done((bf16[128,1024]{1,0:T(8,128)(2,1)S(1)}, bf16[128,1024]{1,0:T(8,128)(2,1)S(1)}, u32[]{:S(2)}, u32[]{:S(2)}) %collective-permute-start.6) | collective-permute-done | bytes 262176 | tf_op jit(solution)/shard_map/ppermute | solution.py:22
  27.1 1.7 %collective-permute-start.8 = (bf16[128,1024]{1,0:T(8,128)(2,1)S(1)}, bf16[128,1024]{1,0:T(8,128)(2,1)S(1)}, u32[]{:S(2)}, u32[]{:S(2)}) collective-permute-start(bf16[128,1024]{1,0:T(8,128)(2,1)S(1)} %collective-permute-done.6.refs_10_), channel_id=1, source_target_pairs={{0,16},{16,0},{32,48},{48,32},{64,80},{80,64},{96,112},{112,96},{1... | collective-permute-start | bytes 786440 | tf_op jit(solution)/shard_map/ppermute | solution.py:22
  28.8 0.3 convolution_convert_fusion.8.refs_7_
  29.1 0.9 collective-permute-done.5.refs_9_
  30.1 1.9 %collective-permute-start.7 = (bf16[128,1024]{1,0:T(8,128)(2,1)S(1)}, bf16[128,1024]{1,0:T(8,128)(2,1)}, u32[]{:S(2)}, u32[]{:S(2)}) collective-permute-start(bf16[128,1024]{1,0:T(8,128)(2,1)S(1)} %collective-permute-done.5.refs_9_), channel_id=1, source_target_pairs={{0,16},{16,0},{32,48},{48,32},{64,80},{80,64},{96,112},{112,96},{1... | collective-permute-start | bytes 786440 | tf_op jit(solution)/shard_map/ppermute | solution.py:22
  32.0 0.3 convolution_convert_fusion.9.refs_6_
  32.3 2.4 %collective-permute-done.8.refs_12_ = bf16[128,1024]{1,0:T(8,128)(2,1)S(1)} collective-permute-done((bf16[128,1024]{1,0:T(8,128)(2,1)S(1)}, bf16[128,1024]{1,0:T(8,128)(2,1)S(1)}, u32[]{:S(2)}, u32[]{:S(2)}) %collective-permute-start.8) | collective-permute-done | bytes 262176 | tf_op jit(solution)/shard_map/ppermute | solution.py:22
  34.7 5.5 %all-to-all-start = ((bf16[8,256,128]{2,1,0:T(8,128)(2,1)}), bf16[8,256,128]{2,1,0:T(8,128)(2,1)S(1)}, u32[]{:S(2)}, u32[]{:S(2)}) async-start(bf16[8,256,128]{2,1,0:T(8,128)(2,1)} %get-tuple-element.32), calls=%async_computation | async-start | bytes 1048576 | tf_op jit(solution)/shard_map/all_to_all | solution.py:30
  40.2 0.3 convolution_convert_fusion.6.refs_9_
  40.5 0.0 copy-start.3
  40.5 0.0 copy-start.4
  40.6 1.5 %convolution_convert_fusion.refs_5_ = bf16[256,384]{1,0:T(8,128)(2,1)S(1)} fusion(bf16[256,1024]{1,0:T(8,128)(2,1)} %collective-permute-done.4.refs_8_, bf16[1024,384]{1,0:T(8,128)(2,1)S(1)} %copy-done.7), kind=kOutput, calls=%fused_computation | convolution fusion | flops 201424896 | bytes 1507328 | tf_op jit(solution)/shard_map/dot_general | solution.py:34
  42.0 1.2 convolution_convert_fusion.7.refs_8_
  43.3 0.0 collective-permute-done.3.refs_7_
  43.3 1.5 %convolution_convert_fusion.1.refs_4_ = bf16[256,384]{1,0:T(8,128)(2,1)S(1)} fusion(bf16[256,1024]{1,0:T(8,128)(2,1)} %collective-permute-done.3.refs_7_, bf16[1024,384]{1,0:T(8,128)(2,1)S(1)} %copy-done.7), kind=kOutput, calls=%fused_computation.1 | convolution fusion | flops 201424896 | bytes 1507328 | tf_op jit(solution)/shard_map/dot_general | solution.py:34
  44.8 3.6 %all-to-all-done.refs_10_ = bf16[8,256,128]{2,1,0:T(8,128)(2,1)S(1)} async-done(((bf16[8,256,128]{2,1,0:T(8,128)(2,1)}), bf16[8,256,128]{2,1,0:T(8,128)(2,1)S(1)}, u32[]{:S(2)}, u32[]{:S(2)}) %all-to-all-start) | async-done | bytes 524320 | tf_op jit(solution)/shard_map/all_to_all | solution.py:30
  48.4 19.9 %attention.1 = (bf16[2048,128]{1,0:T(8,128)(2,1)}, bf16[2048,384]{1,0:T(8,128)(2,1)}) custom-call(s32[2]{0:T(128)S(1)} %copy-done.4, bf16[256,384]{1,0:T(8,128)(2,1)S(1)} %convolution_convert_fusion.5.refs_0_, bf16[256,384]{1,0:T(8,128)(2,1)S(1)} %convolution_convert_fusion.4.refs_1_, bf16[256,384]{1,0:T(8,128)(2,1)S(1)} %convolution_convert_fusion.3.refs_2_, ...), custom_call_target="tpu_custom_call" | custom-call | tf_op jit(solution)/shard_map/attention/pallas_call | solution.py:194
  68.3 3.5 %all-to-all-start.1 = ((bf16[8,256,128]{2,1,0:T(8,128)(2,1)}), bf16[8,256,128]{2,1,0:T(8,128)(2,1)S(1)}, u32[]{:S(2)}, u32[]{:S(2)}) async-start(bf16[8,256,128]{2,1,0:T(8,128)(2,1)} %bitcast.5), calls=%async_computation.1 | async-start | bytes 1048576 | tf_op jit(solution)/shard_map/all_to_all | solution.py:30
  71.8 0.0 copy-start
  71.8 0.0 copy-start.5
  71.8 7.1 %projection_gradient.1 = (f32[512,384]{1,0:T(8,128)}, bf16[528,384]{1,0:T(8,128)(2,1)}, f32[8,128]{1,0:T(8,128)}) custom-call(s32[2]{0:T(128)} %pad_add_fusion.refs_0_.pos, bf16[2048,384]{1,0:T(8,128)(2,1)} %get-tuple-element.34.refs_1_, bf16[1024,384]{1,0:T(8,128)(2,1)} %get-tuple-element.30.refs_2_, bf16[256,1024]{1,0:T(8,128)(2,1)} %layernorm.1.refs_3_, ...), custom_call_target="tpu_custom_call" | custom-call | tf_op jit(solution)/shard_map/projection_gradient/pallas_call | solution.py:84
  79.0 0.9 all-to-all-done.1.refs_1_
  79.9 0.0 collective-permute-start.10
  79.9 0.5 collective-permute-start.11
  80.4 2.1 %collective-permute-done.11.refs_6_ = bf16[528,384]{1,0:T(8,128)(2,1)S(1)} collective-permute-done((bf16[528,384]{1,0:T(8,128)(2,1)}, bf16[528,384]{1,0:T(8,128)(2,1)S(1)}, u32[]{:S(2)}, u32[]{:S(2)}) %collective-permute-start.11) | collective-permute-done | bytes 405536 | tf_op jit(solution)/shard_map/ppermute | solution.py:26
  82.5 0.0 collective-permute-done.10.refs_3_
  82.5 1.1 copy-done.2
  83.6 0.7 copy-done.6
  84.3 3.8 %output_gradient.1 = (bf16[272,640]{1,0:T(8,128)(2,1)}, bf16[256,768]{1,0:T(8,128)(2,1)S(1)}, f32[128,1408]{1,0:T(8,128)S(1)}, f32[128,1408]{1,0:T(8,128)S(1)}, f32[8,128]{1,0:T(8,128)S(1)}) custom-call(s32[2]{0:T(128)S(1)} %copy-done.5, bf16[8,256,128]{2,1,0:T(8,128)(2,1)S(1)} %all-to-all-done.1.refs_1_, bf16[256,1024]{1,0:T(8,128)(2,1)S(1)} %bitcast.36, ...), custom_call_target="tpu_custom_call" | custom-call | tf_op jit(solution)/shard_map/output_gradient/pallas_call | solution.py:84
  88.1 2.8 %collective-permute-start.13 = (bf16[256,768]{1,0:T(8,128)(2,1)S(1)}, bf16[256,768]{1,0:T(8,128)(2,1)S(1)}, u32[]{:S(2)}, u32[]{:S(2)}) collective-permute-start(bf16[256,768]{1,0:T(8,128)(2,1)S(1)} %get-tuple-element.43), channel_id=1, source_target_pairs={{0,12},{1,13},{2,14},{3,15},{4,8},{5,9},{6,10},{7,11},{8,4},{9,5},... | collective-permute-start | bytes 1179656 | tf_op jit(solution)/shard_map/ppermute | solution.py:26
  91.0 0.2 collective-permute-start.12
  91.2 4.9 %all-to-all-start.2 = ((bf16[8,256,384]{2,1,0:T(8,128)(2,1)}), bf16[8,256,384]{2,1,0:T(8,128)(2,1)}, u32[]{:S(2)}, u32[]{:S(2)}) async-start(bf16[8,256,384]{2,1,0:T(8,128)(2,1)} %bitcast.7), calls=%async_computation.2 | async-start | bytes 3145728 | tf_op jit(solution)/shard_map/all_to_all | solution.py:30
  96.1 3.5 %layer_out.1 = bf16[256,1024]{1,0:T(8,128)(2,1)} custom-call(bf16[256,1024]{1,0:T(8,128)(2,1)} %bitcast.38, bf16[8,256,128]{2,1,0:T(8,128)(2,1)} %copy-done.1, bf16[1024,1024]{1,0:T(8,128)(2,1)} %refs_2_.3), custom_call_target="tpu_custom_call" | custom-call | tf_op jit(solution)/shard_map/layer_out/pallas_call | solution.py:84
  99.5 1.5 %collective-permute-done.12 = bf16[272,640]{1,0:T(8,128)(2,1)S(1)} collective-permute-done((bf16[272,640]{1,0:T(8,128)(2,1)}, bf16[272,640]{1,0:T(8,128)(2,1)S(1)}, u32[]{:S(2)}, u32[]{:S(2)}) %collective-permute-start.12) | collective-permute-done | bytes 348192 | tf_op jit(solution)/shard_map/ppermute | solution.py:26
  101.1 0.0 collective-permute-done.13
  101.2 2.3 %collective-permute-start.14 = (bf16[136,640]{1,0:T(8,128)(2,1)S(1)}, bf16[136,640]{1,0:T(8,128)(2,1)S(1)}, u32[]{:S(2)}, u32[]{:S(2)}) collective-permute-start(bf16[136,640]{1,0:T(8,128)(2,1)S(1)} %pad_maximum_fusion.3), channel_id=1, source_target_pairs={{0,12},{1,13},{2,14},{3,15},{4,8},{5,9},{6,10},{7,11},{8,4},{9,5},... | collective-permute-start | bytes 522248 | tf_op jit(solution)/shard_map/ppermute | solution.py:26
  103.5 0.1 collective-permute-start.15
  103.6 4.3 %collective-permute-done.14 = bf16[136,640]{1,0:T(8,128)(2,1)S(1)} collective-permute-done((bf16[136,640]{1,0:T(8,128)(2,1)S(1)}, bf16[136,640]{1,0:T(8,128)(2,1)S(1)}, u32[]{:S(2)}, u32[]{:S(2)}) %collective-permute-start.14) | collective-permute-done | bytes 174112 | tf_op jit(solution)/shard_map/ppermute | solution.py:26
  108.0 1.5 %collective-permute-done.15 = bf16[128,768]{1,0:T(8,128)(2,1)S(1)} collective-permute-done((bf16[128,768]{1,0:T(8,128)(2,1)S(1)}, bf16[128,768]{1,0:T(8,128)(2,1)S(1)}, u32[]{:S(2)}, u32[]{:S(2)}) %collective-permute-start.15) | collective-permute-done | bytes 196640 | tf_op jit(solution)/shard_map/ppermute | solution.py:26
  109.5 0.1 maximum_add_fusion
  109.6 3.7 %collective-permute-start.16 = (bf16[72,1408]{1,0:T(8,128)(2,1)S(1)}, bf16[72,1408]{1,0:T(8,128)(2,1)S(1)}, u32[]{:S(2)}, u32[]{:S(2)}) collective-permute-start(bf16[72,1408]{1,0:T(8,128)(2,1)S(1)} %pad_maximum_fusion.2), channel_id=1, source_target_pairs={{0,2},{1,3},{2,0},{3,1},{4,6},{5,7},{6,4},{7,5},{8,10},{9,11},{10,... | collective-permute-start | bytes 608264 | tf_op jit(solution)/shard_map/ppermute | solution.py:26
  113.3 8.0 %collective-permute-done.16 = bf16[72,1408]{1,0:T(8,128)(2,1)S(1)} collective-permute-done((bf16[72,1408]{1,0:T(8,128)(2,1)S(1)}, bf16[72,1408]{1,0:T(8,128)(2,1)S(1)}, u32[]{:S(2)}, u32[]{:S(2)}) %collective-permute-start.16) | collective-permute-done | bytes 202784 | tf_op jit(solution)/shard_map/ppermute | solution.py:26
  121.4 0.0 all-to-all-done.2.refs_1_
  121.4 0.7 pad_maximum_fusion.1
  122.1 4.8 %all-to-all-start.3 = ((bf16[8,8,1664]{2,1,0:T(8,128)(2,1)}), bf16[8,8,1664]{2,1,0:T(8,128)(2,1)S(1)}, u32[]{:S(2)}, u32[]{:S(2)}) async-start(bf16[8,8,1664]{2,1,0:T(8,128)(2,1)} %pad_maximum_fusion.1), calls=%async_computation.3 | async-start | bytes 425984 | tf_op jit(solution)/shard_map/all_to_all | solution.py:30
  126.9 8.7 %frame_gradient.1 = bf16[256,1024]{1,0:T(8,128)(2,1)} custom-call(bf16[256,1024]{1,0:T(8,128)(2,1)} %bitcast.39, bf16[8,256,384]{2,1,0:T(8,128)(2,1)} %all-to-all-done.2.refs_1_, bf16[256,1024]{1,0:T(8,128)(2,1)} %bitcast.35, f32[1,1024]{1,0:T(1,128)} %bitcast.45, bf16[1024,3072]{1,0:T(8,128)(2,1)} %refs_4_.1), custom_call_target="tpu_custom_call" | custom-call | tf_op jit(solution)/shard_map/frame_gradient/pallas_call | solution.py:84
  135.6 0.7 finish.1
  (49 shorter events, 0.4 us)
Async XLA Ops:
  2.8 15.2 %collective-permute-start.2 = (bf16[256,1024]{1,0:T(8,128)(2,1)}, bf16[256,1024]{1,0:T(8,128)(2,1)S(1)}, u32[]{:S(2)}, u32[]{:S(2)}) collective-permute-start(bf16[256,1024]{1,0:T(8,128)(2,1)} %layernorm.1.refs_3_), channel_id=1, source_target_pairs={{0,96},{16,112},{32,64},{48,80},{64,32},{80,48},{96,0},{112,16},{1... | collective-permute-start | bytes 1572872 | tf_op jit(solution)/shard_map/ppermute | solution.py:22
  5.9 13.6 %collective-permute-start.1 = (bf16[256,1024]{1,0:T(8,128)(2,1)}, bf16[256,1024]{1,0:T(8,128)(2,1)S(1)}, u32[]{:S(2)}, u32[]{:S(2)}) collective-permute-start(bf16[256,1024]{1,0:T(8,128)(2,1)} %layernorm.1.refs_3_), channel_id=1, source_target_pairs={{0,32},{16,48},{32,0},{48,16},{64,96},{80,112},{96,64},{112,80},{1... | collective-permute-start | bytes 1572872 | tf_op jit(solution)/shard_map/ppermute | solution.py:22
  6.1 15.2 %collective-permute-start = (bf16[256,1024]{1,0:T(8,128)(2,1)}, bf16[256,1024]{1,0:T(8,128)(2,1)}, u32[]{:S(2)}, u32[]{:S(2)}) collective-permute-start(bf16[256,1024]{1,0:T(8,128)(2,1)} %layernorm.1.refs_3_), channel_id=1, source_target_pairs={{0,16},{16,0},{32,48},{48,32},{64,80},{80,64},{96,112},{112,96},{1... | collective-permute-start | bytes 1572872 | tf_op jit(solution)/shard_map/ppermute | solution.py:22
  8.0 24.3 %collective-permute-start.9 = (bf16[256,1024]{1,0:T(8,128)(2,1)}, bf16[256,1024]{1,0:T(8,128)(2,1)S(1)}, u32[]{:S(2)}, u32[]{:S(2)}) collective-permute-start(bf16[256,1024]{1,0:T(8,128)(2,1)} %bitcast.33), channel_id=1, source_target_pairs={{0,1},{1,0},{2,3},{3,2},{4,5},{5,4},{6,7},{7,6},{8,9},{9,8},{10,11... | collective-permute-start | bytes 1572872 | tf_op jit(solution)/shard_map/ppermute | solution.py:26
  8.6 4.6 %copy-start.8 = (bf16[256,1024]{1,0:T(8,128)(2,1)S(1)}, bf16[256,1024]{1,0:T(8,128)(2,1)}, u32[]{:S(2)}) copy-start(bf16[256,1024]{1,0:T(8,128)(2,1)} %layernorm.1.refs_3_) | copy-start | bytes 1572868
  13.2 9.7 %copy-start.7 = (bf16[1024,384]{1,0:T(8,128)(2,1)S(1)}, bf16[1024,384]{1,0:T(8,128)(2,1)}, u32[]{:S(2)}) copy-start(bf16[1024,384]{1,0:T(8,128)(2,1)} %get-tuple-element.30.refs_2_) | copy-start | bytes 2359300
  18.1 4.8 %copy-start.9 = (bf16[256,1024]{1,0:T(8,128)(2,1)}, bf16[256,1024]{1,0:T(8,128)(2,1)S(1)}, u32[]{:S(2)}) copy-start(bf16[256,1024]{1,0:T(8,128)(2,1)S(1)} %collective-permute-done.2.refs_6_) | copy-start | bytes 1572868
  18.1 9.0 %collective-permute-start.6 = (bf16[128,1024]{1,0:T(8,128)(2,1)S(1)}, bf16[128,1024]{1,0:T(8,128)(2,1)S(1)}, u32[]{:S(2)}, u32[]{:S(2)}) collective-permute-start(bf16[128,1024]{1,0:T(8,128)(2,1)S(1)} %slice.99), channel_id=1, source_target_pairs={{0,32},{16,48},{32,0},{48,16},{64,96},{80,112},{96,64},{112,80},{1... | collective-permute-start | bytes 786440 | tf_op jit(solution)/shard_map/ppermute | solution.py:22
  19.5 5.7 %copy-start.10 = (bf16[256,1024]{1,0:T(8,128)(2,1)}, bf16[256,1024]{1,0:T(8,128)(2,1)S(1)}, u32[]{:S(2)}) copy-start(bf16[256,1024]{1,0:T(8,128)(2,1)S(1)} %collective-permute-done.1.refs_5_) | copy-start | bytes 1572868
  19.5 10.5 %collective-permute-start.5 = (bf16[128,1024]{1,0:T(8,128)(2,1)S(1)}, bf16[128,1024]{1,0:T(8,128)(2,1)S(1)}, u32[]{:S(2)}, u32[]{:S(2)}) collective-permute-start(bf16[128,1024]{1,0:T(8,128)(2,1)S(1)} %slice.98), channel_id=1, source_target_pairs={{0,96},{16,112},{32,64},{48,80},{64,32},{80,48},{96,0},{112,16},{1... | collective-permute-start | bytes 786440 | tf_op jit(solution)/shard_map/ppermute | solution.py:22
  21.3 19.3 %collective-permute-start.4 = (bf16[256,1024]{1,0:T(8,128)(2,1)}, bf16[256,1024]{1,0:T(8,128)(2,1)}, u32[]{:S(2)}, u32[]{:S(2)}) collective-permute-start(bf16[256,1024]{1,0:T(8,128)(2,1)} %collective-permute-done.refs_4_), channel_id=1, source_target_pairs={{0,96},{16,112},{32,64},{48,80},{64,32},{80,48},{96,0},{112,16},{1... | collective-permute-start | bytes 1572872 | tf_op jit(solution)/shard_map/ppermute | solution.py:22
  22.9 20.4 %collective-permute-start.3 = (bf16[256,1024]{1,0:T(8,128)(2,1)}, bf16[256,1024]{1,0:T(8,128)(2,1)}, u32[]{:S(2)}, u32[]{:S(2)}) collective-permute-start(bf16[256,1024]{1,0:T(8,128)(2,1)} %collective-permute-done.refs_4_), channel_id=1, source_target_pairs={{0,32},{16,48},{32,0},{48,16},{64,96},{80,112},{96,64},{112,80},{1... | collective-permute-start | bytes 1572872 | tf_op jit(solution)/shard_map/ppermute | solution.py:22
  27.1 5.2 %copy-start.11 = (bf16[128,1024]{1,0:T(8,128)(2,1)}, bf16[128,1024]{1,0:T(8,128)(2,1)S(1)}, u32[]{:S(2)}) copy-start(bf16[128,1024]{1,0:T(8,128)(2,1)S(1)} %collective-permute-done.6.refs_10_) | copy-start | bytes 786436
  27.1 7.7 %collective-permute-start.8 = (bf16[128,1024]{1,0:T(8,128)(2,1)S(1)}, bf16[128,1024]{1,0:T(8,128)(2,1)S(1)}, u32[]{:S(2)}, u32[]{:S(2)}) collective-permute-start(bf16[128,1024]{1,0:T(8,128)(2,1)S(1)} %collective-permute-done.6.refs_10_), channel_id=1, source_target_pairs={{0,16},{16,0},{32,48},{48,32},{64,80},{80,64},{96,112},{112,96},{1... | collective-permute-start | bytes 786440 | tf_op jit(solution)/shard_map/ppermute | solution.py:22
  30.1 12.0 %copy-start.12 = (bf16[128,1024]{1,0:T(8,128)(2,1)}, bf16[128,1024]{1,0:T(8,128)(2,1)S(1)}, u32[]{:S(2)}) copy-start(bf16[128,1024]{1,0:T(8,128)(2,1)S(1)} %collective-permute-done.5.refs_9_) | copy-start | bytes 786436
  30.1 12.0 %collective-permute-start.7 = (bf16[128,1024]{1,0:T(8,128)(2,1)S(1)}, bf16[128,1024]{1,0:T(8,128)(2,1)}, u32[]{:S(2)}, u32[]{:S(2)}) collective-permute-start(bf16[128,1024]{1,0:T(8,128)(2,1)S(1)} %collective-permute-done.5.refs_9_), channel_id=1, source_target_pairs={{0,16},{16,0},{32,48},{48,32},{64,80},{80,64},{96,112},{112,96},{1... | collective-permute-start | bytes 786440 | tf_op jit(solution)/shard_map/ppermute | solution.py:22
  34.7 5.8 %copy-start.13 = (bf16[128,1024]{1,0:T(8,128)(2,1)}, bf16[128,1024]{1,0:T(8,128)(2,1)S(1)}, u32[]{:S(2)}) copy-start(bf16[128,1024]{1,0:T(8,128)(2,1)S(1)} %collective-permute-done.8.refs_12_) | copy-start | bytes 786436
  34.7 13.7 %all-to-all-start = ((bf16[8,256,128]{2,1,0:T(8,128)(2,1)}), bf16[8,256,128]{2,1,0:T(8,128)(2,1)S(1)}, u32[]{:S(2)}, u32[]{:S(2)}) async-start(bf16[8,256,128]{2,1,0:T(8,128)(2,1)} %get-tuple-element.32), calls=%async_computation | async-start | bytes 1048576 | tf_op jit(solution)/shard_map/all_to_all | solution.py:30
  40.5 7.9 %copy-start.3 = (s32[1,2048]{1,0:T(1,128)S(1)}, s32[1,2048]{1,0:T(1,128)}, u32[]{:S(2)}) copy-start(s32[1,2048]{1,0:T(1,128)} %refs_11_.1) | copy-start | bytes 24580
  40.5 7.9 %copy-start.4 = (s32[2]{0:T(128)S(1)}, s32[2]{0:T(128)}, u32[]{:S(2)}) copy-start(s32[2]{0:T(128)} %pad_add_fusion.refs_0_.pos) | copy-start | bytes 28
  68.3 11.6 %all-to-all-start.1 = ((bf16[8,256,128]{2,1,0:T(8,128)(2,1)}), bf16[8,256,128]{2,1,0:T(8,128)(2,1)S(1)}, u32[]{:S(2)}, u32[]{:S(2)}) async-start(bf16[8,256,128]{2,1,0:T(8,128)(2,1)} %bitcast.5), calls=%async_computation.1 | async-start | bytes 1048576 | tf_op jit(solution)/shard_map/all_to_all | solution.py:30
  71.8 10.7 %copy-start = (bf16[1,256,1024]{2,1,0:T(8,128)(2,1)S(1)}, bf16[1,256,1024]{2,1,0:T(8,128)(2,1)}, u32[]{:S(2)}) copy-start(bf16[1,256,1024]{2,1,0:T(8,128)(2,1)} %param.11) | copy-start | bytes 1572868
  71.8 10.7 %copy-start.5 = (s32[2]{0:T(128)S(1)}, s32[2]{0:T(128)}, u32[]{:S(2)}) copy-start(s32[2]{0:T(128)} %pad_add_fusion.refs_0_.pos) | copy-start | bytes 28
  79.9 11.3 %copy-start.1 = (bf16[8,256,128]{2,1,0:T(8,128)(2,1)}, bf16[8,256,128]{2,1,0:T(8,128)(2,1)S(1)}, u32[]{:S(2)}) copy-start(bf16[8,256,128]{2,1,0:T(8,128)(2,1)S(1)} %all-to-all-done.1.refs_1_) | copy-start | bytes 1572868
  79.9 2.6 %collective-permute-start.10 = (bf16[8,256,128]{2,1,0:T(8,128)(2,1)S(1)}, bf16[8,256,128]{2,1,0:T(8,128)(2,1)S(1)}, u32[]{:S(2)}, u32[]{:S(2)}) collective-permute-start(bf16[8,256,128]{2,1,0:T(8,128)(2,1)S(1)} %all-to-all-done.1.refs_1_), channel_id=1, source_target_pairs={{0,1},{1,0},{2,3},{3,2},{4,5},{5,4},{6,7},{7,6},{8,9},{9,8},{10,11... | collective-permute-start | bytes 1572872 | tf_op jit(solution)/shard_map/ppermute | solution.py:26
  79.9 2.6 %collective-permute-start.11 = (bf16[528,384]{1,0:T(8,128)(2,1)}, bf16[528,384]{1,0:T(8,128)(2,1)S(1)}, u32[]{:S(2)}, u32[]{:S(2)}) collective-permute-start(bf16[528,384]{1,0:T(8,128)(2,1)} %get-tuple-element.40), channel_id=1, source_target_pairs={{0,1},{1,0},{2,3},{3,2},{4,5},{5,4},{6,7},{7,6},{8,9},{9,8},{10,11... | collective-permute-start | bytes 1216520 | tf_op jit(solution)/shard_map/ppermute | solution.py:26
  82.5 1.1 copy-start.2
  83.6 0.7 copy-start.6
  88.1 13.0 %collective-permute-start.13 = (bf16[256,768]{1,0:T(8,128)(2,1)S(1)}, bf16[256,768]{1,0:T(8,128)(2,1)S(1)}, u32[]{:S(2)}, u32[]{:S(2)}) collective-permute-start(bf16[256,768]{1,0:T(8,128)(2,1)S(1)} %get-tuple-element.43), channel_id=1, source_target_pairs={{0,12},{1,13},{2,14},{3,15},{4,8},{5,9},{6,10},{7,11},{8,4},{9,5},... | collective-permute-start | bytes 1179656 | tf_op jit(solution)/shard_map/ppermute | solution.py:26
  91.0 10.1 %collective-permute-start.12 = (bf16[272,640]{1,0:T(8,128)(2,1)}, bf16[272,640]{1,0:T(8,128)(2,1)S(1)}, u32[]{:S(2)}, u32[]{:S(2)}) collective-permute-start(bf16[272,640]{1,0:T(8,128)(2,1)} %get-tuple-element.42), channel_id=1, source_target_pairs={{0,4},{1,5},{2,6},{3,7},{4,0},{5,1},{6,2},{7,3},{8,12},{9,13},{10,... | collective-permute-start | bytes 1044488 | tf_op jit(solution)/shard_map/ppermute | solution.py:26
  91.2 30.2 %all-to-all-start.2 = ((bf16[8,256,384]{2,1,0:T(8,128)(2,1)}), bf16[8,256,384]{2,1,0:T(8,128)(2,1)}, u32[]{:S(2)}, u32[]{:S(2)}) async-start(bf16[8,256,384]{2,1,0:T(8,128)(2,1)} %bitcast.7), calls=%async_computation.2 | async-start | bytes 3145728 | tf_op jit(solution)/shard_map/all_to_all | solution.py:30
  101.2 6.7 %collective-permute-start.14 = (bf16[136,640]{1,0:T(8,128)(2,1)S(1)}, bf16[136,640]{1,0:T(8,128)(2,1)S(1)}, u32[]{:S(2)}, u32[]{:S(2)}) collective-permute-start(bf16[136,640]{1,0:T(8,128)(2,1)S(1)} %pad_maximum_fusion.3), channel_id=1, source_target_pairs={{0,12},{1,13},{2,14},{3,15},{4,8},{5,9},{6,10},{7,11},{8,4},{9,5},... | collective-permute-start | bytes 522248 | tf_op jit(solution)/shard_map/ppermute | solution.py:26
  103.5 5.9 %collective-permute-start.15 = (bf16[128,768]{1,0:T(8,128)(2,1)S(1)}, bf16[128,768]{1,0:T(8,128)(2,1)S(1)}, u32[]{:S(2)}, u32[]{:S(2)}) collective-permute-start(bf16[128,768]{1,0:T(8,128)(2,1)S(1)} %add_convert_fusion), channel_id=1, source_target_pairs={{0,4},{1,5},{2,6},{3,7},{4,0},{5,1},{6,2},{7,3},{8,12},{9,13},{10,... | collective-permute-start | bytes 589832 | tf_op jit(solution)/shard_map/ppermute | solution.py:26
  109.6 11.6 %collective-permute-start.16 = (bf16[72,1408]{1,0:T(8,128)(2,1)S(1)}, bf16[72,1408]{1,0:T(8,128)(2,1)S(1)}, u32[]{:S(2)}, u32[]{:S(2)}) collective-permute-start(bf16[72,1408]{1,0:T(8,128)(2,1)S(1)} %pad_maximum_fusion.2), channel_id=1, source_target_pairs={{0,2},{1,3},{2,0},{3,1},{4,6},{5,7},{6,4},{7,5},{8,10},{9,11},{10,... | collective-permute-start | bytes 608264 | tf_op jit(solution)/shard_map/ppermute | solution.py:26
  122.1 13.5 %all-to-all-start.3 = ((bf16[8,8,1664]{2,1,0:T(8,128)(2,1)}), bf16[8,8,1664]{2,1,0:T(8,128)(2,1)S(1)}, u32[]{:S(2)}, u32[]{:S(2)}) async-start(bf16[8,8,1664]{2,1,0:T(8,128)(2,1)} %pad_maximum_fusion.1), calls=%async_computation.3 | async-start | bytes 425984 | tf_op jit(solution)/shard_map/all_to_all | solution.py:30
